TPU v7x, 512 devices: a whole 4x8x8 slice. The times are simulated.
512 devices in a mesh: blk: 32 (over z, y_lo), off: 16 (over x, y_hi, core).
Axes of the slice: x: 4, y: 8 (y_hi: 2, y_lo: 4; y = y_hi * 4 + y_lo), z: 8, core: 2. Of those that a mesh axis runs over, the one named last changes fastest.
Arguments:
- orbitals: bfloat16 [32, 48, 2304], P('blk'), may hold values from -1.5 to 1.5
Outputs:
- exchange: float32 [32, 48, 2304], P('blk', 'off')
All inputs are finite; a program needn't handle non-finite values.
Results may differ from a plain program's by a relative error of at most 0.00055.
Values may be sent and summed in bfloat16 or wider, within the bound.
A program may use at most 64 MiB of HBM per device.

v0:
```python
import math

import jax
import jax.numpy as jnp
from jax import lax
from jax.sharding import PartitionSpec as P

cell_edge = 59.0
screen_rate = 0.106


def from_behind(block, axis, distance):
    devices = range(lax.axis_size(axis))
    route = [((i - distance) % len(devices), i) for i in devices]
    return lax.ppermute(block, axis, route)


def split_up(x, dim, size):
    dims = x.shape
    blocks = x.reshape(*dims[:dim], size, dims[dim] // size, *dims[dim + 1 :])
    return jnp.moveaxis(blocks, dim, 0)


def summed_on_arrival(x, axis, dim):
    blocks = split_up(x, dim, lax.axis_size(axis))
    arrived = lax.all_to_all(blocks, axis, split_axis=0, concat_axis=0, tiled=True)
    return arrived.sum(axis=0)


def screened_kernel(grid_edge):
    points = jnp.arange(grid_edge, dtype=jnp.int32)
    signed = jnp.where(points > grid_edge // 2, points - grid_edge, points)
    half_points = jnp.arange(grid_edge // 2 + 1, dtype=jnp.int32)
    squared = (
        signed[:, None, None] ** 2 + signed[None, :, None] ** 2 + half_points[None, None, :] ** 2
    )
    wave_sq = squared.astype(jnp.float32) * jnp.float32((2.0 * math.pi / cell_edge) ** 2)
    safe_sq = jnp.where(squared == 0, jnp.float32(1.0), wave_sq)
    screened = 4.0 * math.pi * -jnp.expm1(-safe_sq / (4.0 * screen_rate**2)) / safe_sq
    return jnp.where(squared == 0, jnp.float32(math.pi / screen_rate**2), screened)


def dft_tables(grid_edge):
    points = jnp.arange(grid_edge, dtype=jnp.int32)
    phase = points[:, None] * points[None, :] % grid_edge
    angles = phase.astype(jnp.float32) * jnp.float32(2.0 * math.pi / grid_edge)
    cosine = jnp.cos(angles)
    sine = jnp.sin(angles)
    half_size = grid_edge // 2 + 1
    half_points = points[:half_size]
    weights = jnp.where((half_points == 0) | (half_points == grid_edge // 2), 1.0, 2.0).astype(
        jnp.float32
    )
    weights = weights / jnp.float32(grid_edge**3)
    cos_half = cosine[:, :half_size]
    sin_half = sine[:, :half_size]
    first_table = jnp.stack([cos_half, -sin_half], axis=1)
    forward = jnp.stack([jnp.stack([cosine, -sine]), jnp.stack([sine, cosine])]).transpose(
        0, 2, 1, 3
    )
    backward = jnp.stack([jnp.stack([cosine, sine]), jnp.stack([-sine, cosine])]).transpose(
        0, 2, 1, 3
    )
    back_cos = (cos_half * weights[None, :]).T
    back_sin = (sin_half * weights[None, :]).T
    last_table = jnp.stack([back_cos, -back_sin])
    return (first_table, forward, backward, last_table)


def contract(form, data, table):
    return jnp.einsum(form, data, table, precision=lax.Precision.HIGHEST)


def potential(density, tables, kernel):
    first_table, forward, backward, last_table = tables
    spectrum = contract("pxyz,zck->cpxyk", density, first_table)
    spectrum = contract("cpxyk,cydv->dpxvk", spectrum, forward)
    spectrum = contract("dpxvk,dxeu->epuvk", spectrum, forward)
    spectrum = spectrum * kernel
    spectrum = contract("epuvk,eufx->fpxvk", spectrum, backward)
    spectrum = contract("fpxvk,fvgy->gpxyk", spectrum, backward)
    return contract("gpxyk,gkz->pxyz", spectrum, last_table)


def pair_terms(left_block, right_block, tables, kernel):
    band_count, grid_edge, plane_size = left_block.shape
    right_fields = right_block.astype(jnp.float32)
    right_cubes = right_fields.reshape(band_count, grid_edge, grid_edge, grid_edge)
    home_terms = jnp.zeros(left_block.shape, jnp.float32)
    other_terms = jnp.zeros(left_block.shape, jnp.float32)

    def step(first_band, carry):
        home_acc, other_acc = carry
        left_band = lax.dynamic_index_in_dim(left_block, first_band, 0, keepdims=False).astype(
            jnp.float32
        )
        densities = left_band.reshape(1, grid_edge, grid_edge, grid_edge) * right_cubes
        fields = potential(densities, tables, kernel).reshape(band_count, grid_edge, plane_size)
        home_row = jnp.sum(right_fields * fields, axis=0)
        home_acc = lax.dynamic_update_index_in_dim(home_acc, home_row, first_band, 0)
        return (home_acc, other_acc)

    return lax.fori_loop(0, band_count, step, (home_terms, other_terms))


def on_device(orbitals):
    band_count, grid_edge, plane_size = orbitals.shape
    cycle_size = lax.axis_size("blk")
    digit_count = cycle_size.bit_length() - 1
    offset_group = lax.axis_index("off")
    distance = jnp.where(offset_group == 0, cycle_size // 2, offset_group)
    tables = dft_tables(grid_edge)
    kernel = screened_kernel(grid_edge)
    ahead = orbitals
    for bit_level in range(digit_count):
        arrived = from_behind(ahead, "blk", -(1 << bit_level))
        ahead = jnp.where((distance >> bit_level) % 2 == 1, arrived, ahead)
    behind = orbitals
    for bit_level in range(digit_count):
        arrived = from_behind(behind, "blk", 1 << bit_level)
        behind = jnp.where((distance >> bit_level) % 2 == 1, arrived, behind)
    behind = jnp.where(offset_group == 0, orbitals, behind)
    ahead_terms, unused_ahead = pair_terms(orbitals, ahead, tables, kernel)
    behind_terms, unused_behind = pair_terms(orbitals, behind, tables, kernel)
    summed = ahead_terms + behind_terms
    summed = jnp.float32(-0.25) * summed
    return summed_on_arrival(summed, "off", 1)


def solution(mesh):
    return jax.shard_map(
        on_device,
        mesh=mesh,
        in_specs=(P("blk", None, None),),
        out_specs=P("blk", "off", None),
        check_vma=False,
    )
```

profile of v0, /device:TPU:9, one launch (start us, length us, event | category | flops | bytes accessed | tf_op | source)
XLA Modules:
  0.0 164.7 jit_solution(8310041016018848829)
XLA Ops:
  0.0 3.3 %collective-permute-start.5 = (bf16[1,48,2304]{2,1,0:T(8,128)(2,1)}, bf16[1,48,2304]{2,1,0:T(8,128)(2,1)S(1)}, u32[]{:S(2)}, u32[]{:S(2)}) collective-permute-start(bf16[1,48,2304]{2,1,0:T(8,128)(2,1)} %param.1), channel_id=1, source_target_pairs={{496,0},{0,16},{16,32},{32,48},{48,64},{64,80},{80,96},{96,112},{1... | collective-permute-start | bytes 663560 | tf_op jit(solution)/shard_map/ppermute | solution.py:15
  3.3 2.1 %collective-permute-start = (bf16[1,48,2304]{2,1,0:T(8,128)(2,1)}, bf16[1,48,2304]{2,1,0:T(8,128)(2,1)S(1)}, u32[]{:S(2)}, u32[]{:S(2)}) collective-permute-start(bf16[1,48,2304]{2,1,0:T(8,128)(2,1)} %param.1), channel_id=1, source_target_pairs={{16,0},{32,16},{48,32},{64,48},{80,64},{96,80},{112,96},{128,112},... | collective-permute-start | bytes 663560 | tf_op jit(solution)/shard_map/ppermute | solution.py:15
  8.0 8.9 %collective-permute-done = bf16[1,48,2304]{2,1,0:T(8,128)(2,1)S(1)} collective-permute-done((bf16[1,48,2304]{2,1,0:T(8,128)(2,1)}, bf16[1,48,2304]{2,1,0:T(8,128)(2,1)S(1)}, u32[]{:S(2)}, u32[]{:S(2)}) %collective-permute-start) | collective-permute-done | bytes 221216 | tf_op jit(solution)/shard_map/ppermute | solution.py:15
  17.0 1.9 %collective-permute-start.6 = (bf16[1,48,2304]{2,1,0:T(8,128)(2,1)S(1)}, bf16[1,48,2304]{2,1,0:T(8,128)(2,1)S(1)}, u32[]{:S(2)}, u32[]{:S(2)}) collective-permute-start(bf16[1,48,2304]{2,1,0:T(8,128)(2,1)S(1)} %get-tuple-element.49), channel_id=1, source_target_pairs={{480,0},{496,16},{0,32},{16,48},{32,64},{48,80},{64,96},{80,112},{... | collective-permute-start | bytes 663560 | tf_op jit(solution)/shard_map/ppermute | solution.py:15
  18.9 10.1 %collective-permute-start.1 = (bf16[1,48,2304]{2,1,0:T(8,128)(2,1)S(1)}, bf16[1,48,2304]{2,1,0:T(8,128)(2,1)S(1)}, u32[]{:S(2)}, u32[]{:S(2)}) collective-permute-start(bf16[1,48,2304]{2,1,0:T(8,128)(2,1)S(1)} %get-tuple-element.50), channel_id=1, source_target_pairs={{32,0},{48,16},{64,32},{80,48},{96,64},{112,80},{128,96},{144,112}... | collective-permute-start | bytes 663560 | tf_op jit(solution)/shard_map/ppermute | solution.py:15
  29.1 5.5 %collective-permute-done.6 = bf16[1,48,2304]{2,1,0:T(8,128)(2,1)S(1)} collective-permute-done((bf16[1,48,2304]{2,1,0:T(8,128)(2,1)S(1)}, bf16[1,48,2304]{2,1,0:T(8,128)(2,1)S(1)}, u32[]{:S(2)}, u32[]{:S(2)}) %collective-permute-start.6) | collective-permute-done | bytes 221216 | tf_op jit(solution)/shard_map/ppermute | solution.py:15
  34.6 2.6 %collective-permute-start.7 = (bf16[1,48,2304]{2,1,0:T(8,128)(2,1)S(1)}, bf16[1,48,2304]{2,1,0:T(8,128)(2,1)S(1)}, u32[]{:S(2)}, u32[]{:S(2)}) collective-permute-start(bf16[1,48,2304]{2,1,0:T(8,128)(2,1)S(1)} %broadcast_select_fusion.2), channel_id=1, source_target_pairs={{448,0},{464,16},{480,32},{496,48},{0,64},{16,80},{32,96},{48,112}... | collective-permute-start | bytes 663560 | tf_op jit(solution)/shard_map/ppermute | solution.py:15
  37.2 2.1 %collective-permute-done.1 = bf16[1,48,2304]{2,1,0:T(8,128)(2,1)S(1)} collective-permute-done((bf16[1,48,2304]{2,1,0:T(8,128)(2,1)S(1)}, bf16[1,48,2304]{2,1,0:T(8,128)(2,1)S(1)}, u32[]{:S(2)}, u32[]{:S(2)}) %collective-permute-start.1) | collective-permute-done | bytes 221216 | tf_op jit(solution)/shard_map/ppermute | solution.py:15
  39.3 8.8 %collective-permute-start.2 = (bf16[1,48,2304]{2,1,0:T(8,128)(2,1)S(1)}, bf16[1,48,2304]{2,1,0:T(8,128)(2,1)S(1)}, u32[]{:S(2)}, u32[]{:S(2)}) collective-permute-start(bf16[1,48,2304]{2,1,0:T(8,128)(2,1)S(1)} %broadcast_select_fusion.3), channel_id=1, source_target_pairs={{64,0},{80,16},{96,32},{112,48},{128,64},{144,80},{160,96},{176,11... | collective-permute-start | bytes 663560 | tf_op jit(solution)/shard_map/ppermute | solution.py:15
  48.6 1.9 %collective-permute-start.8 = (bf16[1,48,2304]{2,1,0:T(8,128)(2,1)S(1)}, bf16[1,48,2304]{2,1,0:T(8,128)(2,1)S(1)}, u32[]{:S(2)}, u32[]{:S(2)}) collective-permute-start(bf16[1,48,2304]{2,1,0:T(8,128)(2,1)S(1)} %broadcast_select_fusion.4), channel_id=1, source_target_pairs={{384,0},{400,16},{416,32},{432,48},{448,64},{464,80},{480,96},{496... | collective-permute-start | bytes 663560 | tf_op jit(solution)/shard_map/ppermute | solution.py:15
  50.6 1.8 %collective-permute-done.2 = bf16[1,48,2304]{2,1,0:T(8,128)(2,1)S(1)} collective-permute-done((bf16[1,48,2304]{2,1,0:T(8,128)(2,1)S(1)}, bf16[1,48,2304]{2,1,0:T(8,128)(2,1)S(1)}, u32[]{:S(2)}, u32[]{:S(2)}) %collective-permute-start.2) | collective-permute-done | bytes 221216 | tf_op jit(solution)/shard_map/ppermute | solution.py:15
  52.4 3.7 %collective-permute-start.3 = (bf16[1,48,2304]{2,1,0:T(8,128)(2,1)S(1)}, bf16[1,48,2304]{2,1,0:T(8,128)(2,1)S(1)}, u32[]{:S(2)}, u32[]{:S(2)}) collective-permute-start(bf16[1,48,2304]{2,1,0:T(8,128)(2,1)S(1)} %broadcast_select_fusion.5), channel_id=1, source_target_pairs={{128,0},{144,16},{160,32},{176,48},{192,64},{208,80},{224,96},{240... | collective-permute-start | bytes 663560 | tf_op jit(solution)/shard_map/ppermute | solution.py:15
  56.1 8.1 %collective-permute-done.8 = bf16[1,48,2304]{2,1,0:T(8,128)(2,1)S(1)} collective-permute-done((bf16[1,48,2304]{2,1,0:T(8,128)(2,1)S(1)}, bf16[1,48,2304]{2,1,0:T(8,128)(2,1)S(1)}, u32[]{:S(2)}, u32[]{:S(2)}) %collective-permute-start.8) | collective-permute-done | bytes 221216 | tf_op jit(solution)/shard_map/ppermute | solution.py:15
  64.3 2.4 %collective-permute-start.9 = (bf16[1,48,2304]{2,1,0:T(8,128)(2,1)S(1)}, bf16[1,48,2304]{2,1,0:T(8,128)(2,1)S(1)}, u32[]{:S(2)}, u32[]{:S(2)}) collective-permute-start(bf16[1,48,2304]{2,1,0:T(8,128)(2,1)S(1)} %broadcast_select_fusion.6), channel_id=1, source_target_pairs={{256,0},{272,16},{288,32},{304,48},{320,64},{336,80},{352,96},{368... | collective-permute-start | bytes 663560 | tf_op jit(solution)/shard_map/ppermute | solution.py:15
  66.7 6.8 %collective-permute-start.4 = (bf16[1,48,2304]{2,1,0:T(8,128)(2,1)S(1)}, bf16[1,48,2304]{2,1,0:T(8,128)(2,1)S(1)}, u32[]{:S(2)}, u32[]{:S(2)}) collective-permute-start(bf16[1,48,2304]{2,1,0:T(8,128)(2,1)S(1)} %broadcast_select_fusion.7), channel_id=1, source_target_pairs={{256,0},{272,16},{288,32},{304,48},{320,64},{336,80},{352,96},{368... | collective-permute-start | bytes 663560 | tf_op jit(solution)/shard_map/ppermute | solution.py:15
  73.6 8.9 %collective-permute-done.9 = bf16[1,48,2304]{2,1,0:T(8,128)(2,1)S(1)} collective-permute-done((bf16[1,48,2304]{2,1,0:T(8,128)(2,1)S(1)}, bf16[1,48,2304]{2,1,0:T(8,128)(2,1)S(1)}, u32[]{:S(2)}, u32[]{:S(2)}) %collective-permute-start.9) | collective-permute-done | bytes 221216 | tf_op jit(solution)/shard_map/ppermute | solution.py:15
  82.6 4.7 %collective-permute-done.4 = bf16[1,48,2304]{2,1,0:T(8,128)(2,1)S(1)} collective-permute-done((bf16[1,48,2304]{2,1,0:T(8,128)(2,1)S(1)}, bf16[1,48,2304]{2,1,0:T(8,128)(2,1)S(1)}, u32[]{:S(2)}, u32[]{:S(2)}) %collective-permute-start.4) | collective-permute-done | bytes 221216 | tf_op jit(solution)/shard_map/ppermute | solution.py:15
  89.0 4.2 %convolution_bitcast_fusion = f32[2,48,48,25]{2,3,1,0:T(8,128)S(1)} fusion(f32[48,48,48,1]{2,1,0,3:T(8,128)S(1)} %reshape.248, f32[48,1,25]{0,2,1:T(8,128)S(1)} %get-tuple-element.70, f32[48,1,25]{0,2,1:T(8,128)S(1)} %get-tuple-element.71), kind=kOutput, calls=%fused_computation | convolution fusion | flops 66357600 | bytes 912768 | tf_op jit(solution)/shard_map/while/body/eval_jaxpr/pxyz,zck->cpxyk/dot_general | solution.py:71
  93.2 2.8 %convolution_bitcast_fusion.6 = f32[2,48,48,25,1]{1,2,3,0,4:T(8,128)S(1)} fusion(f32[2,48,48,25]{2,3,1,0:T(8,128)S(1)} %convolution_bitcast_fusion, f32[1,2,48,48]{2,3,0,1:T(8,128)S(1)} %get-tuple-element.54, f32[1,2,48,48]{2,3,0,1:T(8,128)S(1)} %get-tuple-element.72), kind=kOutput, calls=%fused_computation.6 | convolution fusion | flops 132719616 | bytes 958464 | tf_op jit(solution)/shard_map/while/body/eval_jaxpr/cpxyk,cydv->dpxvk/dot_general | solution.py:71
  96.0 2.1 %fusion.3 = f32[2,48,48,25,1]{2,1,3,0,4:T(8,128)S(1)} fusion(f32[2,48,48,25,1]{1,2,3,0,4:T(8,128)S(1)} %convolution_bitcast_fusion.6, f32[48,48,25]{1,0,2:T(8,128)S(1)} %fusion.10, f32[1,2,48,48]{2,3,0,1:T(8,128)S(1)} %get-tuple-element.54, f32[1,2,48,48]{2,3,0,1:T(8,128)S(1)} %get-tuple-element.72), kind=kOutput, calls=%fused_computation.15 | convolution fusion | flops 132834816 | bytes 1188864 | tf_op jit(solution)/shard_map/while/body/eval_jaxpr/dpxvk,dxeu->epuvk/dot_general | solution.py:71
  99.4 2.1 %convolution_bitcast_fusion.4 = f32[2,48,48,25]{1,2,3,0:T(8,128)S(1)} fusion(f32[2,48,48,25,1]{2,1,0,3,4:T(8,128)S(1)} %convolution_bitcast_fusion.5, f32[2,48,2,48,1]{1,3,2,0,4:T(8,128)S(1)} %copy-done.7), kind=kOutput, calls=%fused_computation.4 | convolution fusion | flops 132710400 | bytes 958464 | tf_op jit(solution)/shard_map/while/body/eval_jaxpr/fpxvk,fvgy->gpxyk/dot_general | solution.py:71
  101.5 1.3 copy.28
  102.9 2.8 %convolution_bitcast_fusion.10 = f32[48,48,48]{2,1,0:T(8,128)S(1)} fusion(f32[2,48,48,25]{2,3,0,1:T(8,128)S(1)} %copy.28, f32[1,25,48]{2,1,0:T(8,128)S(1)} %get-tuple-element.69, f32[1,25,48]{2,1,0:T(8,128)S(1)} %get-tuple-element.68), kind=kOutput, calls=%fused_computation.10 | convolution fusion | flops 66357600 | bytes 912768 | tf_op jit(solution)/shard_map/while/body/eval_jaxpr/gpxyk,gkz->pxyz/dot_general | solution.py:71
  105.7 1.2 reshape.232
  107.0 1.7 %reshape.234 = f32[48,48,48,1]{2,1,0,3:T(8,128)S(1)} reshape(f32[1,48,2304]{2,1,0:T(8,128)} %get-tuple-element.48) | data formatting | bytes 884736 | tf_op jit(solution)/shard_map/while/body/eval_jaxpr/mul | solution.py:97
  108.7 4.2 %convolution_bitcast_fusion.1 = f32[2,48,48,25]{2,3,1,0:T(8,128)S(1)} fusion(f32[48,48,48,1]{2,1,0,3:T(8,128)S(1)} %reshape.234, f32[48,1,25]{0,2,1:T(8,128)S(1)} %copy-done.16, f32[48,1,25]{0,2,1:T(8,128)S(1)} %copy-done.18), kind=kOutput, calls=%fused_computation.1 | convolution fusion | flops 66357600 | bytes 912768 | tf_op jit(solution)/shard_map/while/body/eval_jaxpr/pxyz,zck->cpxyk/dot_general | solution.py:71
  113.0 2.8 %convolution_bitcast_fusion.9 = f32[2,48,48,25,1]{1,2,3,0,4:T(8,128)S(1)} fusion(f32[2,48,48,25]{2,3,1,0:T(8,128)S(1)} %convolution_bitcast_fusion.1, f32[1,2,48,48]{2,3,0,1:T(8,128)S(1)} %get-tuple-element.54, f32[1,2,48,48]{2,3,0,1:T(8,128)S(1)} %get-tuple-element.72), kind=kOutput, calls=%fused_computation.9 | convolution fusion | flops 132719616 | bytes 958464 | tf_op jit(solution)/shard_map/while/body/eval_jaxpr/cpxyk,cydv->dpxvk/dot_general | solution.py:71
  115.8 2.1 %fusion.1 = f32[2,48,48,25,1]{2,1,3,0,4:T(8,128)S(1)} fusion(f32[2,48,48,25,1]{1,2,3,0,4:T(8,128)S(1)} %convolution_bitcast_fusion.9, f32[48,48,25]{1,0,2:T(8,128)S(1)} %fusion.10, f32[1,2,48,48]{2,3,0,1:T(8,128)S(1)} %get-tuple-element.54, f32[1,2,48,48]{2,3,0,1:T(8,128)S(1)} %get-tuple-element.72), kind=kOutput, calls=%fused_computation.13 | convolution fusion | flops 132834816 | bytes 1188864 | tf_op jit(solution)/shard_map/while/body/eval_jaxpr/dpxvk,dxeu->epuvk/dot_general | solution.py:71
  119.1 2.4 %convolution_bitcast_fusion.7 = f32[2,48,48,25]{1,2,3,0:T(8,128)S(1)} fusion(f32[2,48,48,25,1]{2,1,0,3,4:T(8,128)S(1)} %convolution_bitcast_fusion.8, f32[2,48,2,48,1]{1,3,2,0,4:T(8,128)S(1)} %copy-done.8), kind=kOutput, calls=%fused_computation.7 | convolution fusion | flops 132710400 | bytes 958464 | tf_op jit(solution)/shard_map/while/body/eval_jaxpr/fpxvk,fvgy->gpxyk/dot_general | solution.py:71
  121.5 1.4 copy.22
  122.8 2.6 %convolution_bitcast_fusion.11 = f32[48,48,48]{2,1,0:T(8,128)S(1)} fusion(f32[2,48,48,25]{2,3,0,1:T(8,128)S(1)} %copy.22, f32[1,25,48]{2,1,0:T(8,128)S(1)} %get-tuple-element.69, f32[1,25,48]{2,1,0:T(8,128)S(1)} %get-tuple-element.68), kind=kOutput, calls=%fused_computation.11 | convolution fusion | flops 66357600 | bytes 912768 | tf_op jit(solution)/shard_map/while/body/eval_jaxpr/gpxyk,gkz->pxyz/dot_general | solution.py:71
  127.6 36.1 %all_to_all.5 = f32[16,1,3,2304]{3,1,2,0:T(1,128)S(1)} all-to-all(f32[16,1,3,2304]{3,1,2,0:T(1,128)S(1)} %transpose_reshape.3), channel_id=1, replica_groups=mesh['blk'=32,'off'=16] {'off'}, dimensions={0} | all-to-all | bytes 884736 | tf_op jit(solution)/shard_map/all_to_all | solution.py:26
  (69 shorter events, 10.3 us)
Async XLA Ops:
  0.0 16.9 %copy-start.4 = (bf16[1,48,2304]{2,1,0:T(8,128)(2,1)S(1)}, bf16[1,48,2304]{2,1,0:T(8,128)(2,1)}, u32[]{:S(2)}) copy-start(bf16[1,48,2304]{2,1,0:T(8,128)(2,1)} %param.1) | copy-start | bytes 663556
  0.0 8.0 %collective-permute-start.5 = (bf16[1,48,2304]{2,1,0:T(8,128)(2,1)}, bf16[1,48,2304]{2,1,0:T(8,128)(2,1)S(1)}, u32[]{:S(2)}, u32[]{:S(2)}) collective-permute-start(bf16[1,48,2304]{2,1,0:T(8,128)(2,1)} %param.1), channel_id=1, source_target_pairs={{496,0},{0,16},{16,32},{32,48},{48,64},{64,80},{80,96},{96,112},{1... | collective-permute-start | bytes 663560 | tf_op jit(solution)/shard_map/ppermute | solution.py:15
  3.3 13.6 %collective-permute-start = (bf16[1,48,2304]{2,1,0:T(8,128)(2,1)}, bf16[1,48,2304]{2,1,0:T(8,128)(2,1)S(1)}, u32[]{:S(2)}, u32[]{:S(2)}) collective-permute-start(bf16[1,48,2304]{2,1,0:T(8,128)(2,1)} %param.1), channel_id=1, source_target_pairs={{16,0},{32,16},{48,32},{64,48},{80,64},{96,80},{112,96},{128,112},... | collective-permute-start | bytes 663560 | tf_op jit(solution)/shard_map/ppermute | solution.py:15
  6.5 91.6 %copy-start.9 = (f32[2,48,2,48]{1,3,2,0:T(8,128)}, f32[2,48,2,48]{1,3,2,0:T(8,128)S(1)}, u32[]{:S(2)}) copy-start(f32[2,48,2,48]{1,3,2,0:T(8,128)S(1)} %get-tuple-element.52) | copy-start | bytes 110596
  17.0 17.6 %collective-permute-start.6 = (bf16[1,48,2304]{2,1,0:T(8,128)(2,1)S(1)}, bf16[1,48,2304]{2,1,0:T(8,128)(2,1)S(1)}, u32[]{:S(2)}, u32[]{:S(2)}) collective-permute-start(bf16[1,48,2304]{2,1,0:T(8,128)(2,1)S(1)} %get-tuple-element.49), channel_id=1, source_target_pairs={{480,0},{496,16},{0,32},{16,48},{32,64},{48,80},{64,96},{80,112},{... | collective-permute-start | bytes 663560 | tf_op jit(solution)/shard_map/ppermute | solution.py:15
  18.9 20.4 %collective-permute-start.1 = (bf16[1,48,2304]{2,1,0:T(8,128)(2,1)S(1)}, bf16[1,48,2304]{2,1,0:T(8,128)(2,1)S(1)}, u32[]{:S(2)}, u32[]{:S(2)}) collective-permute-start(bf16[1,48,2304]{2,1,0:T(8,128)(2,1)S(1)} %get-tuple-element.50), channel_id=1, source_target_pairs={{32,0},{48,16},{64,32},{80,48},{96,64},{112,80},{128,96},{144,112}... | collective-permute-start | bytes 663560 | tf_op jit(solution)/shard_map/ppermute | solution.py:15
  34.6 14.0 %collective-permute-start.7 = (bf16[1,48,2304]{2,1,0:T(8,128)(2,1)S(1)}, bf16[1,48,2304]{2,1,0:T(8,128)(2,1)S(1)}, u32[]{:S(2)}, u32[]{:S(2)}) collective-permute-start(bf16[1,48,2304]{2,1,0:T(8,128)(2,1)S(1)} %broadcast_select_fusion.2), channel_id=1, source_target_pairs={{448,0},{464,16},{480,32},{496,48},{0,64},{16,80},{32,96},{48,112}... | collective-permute-start | bytes 663560 | tf_op jit(solution)/shard_map/ppermute | solution.py:15
  39.3 13.1 %collective-permute-start.2 = (bf16[1,48,2304]{2,1,0:T(8,128)(2,1)S(1)}, bf16[1,48,2304]{2,1,0:T(8,128)(2,1)S(1)}, u32[]{:S(2)}, u32[]{:S(2)}) collective-permute-start(bf16[1,48,2304]{2,1,0:T(8,128)(2,1)S(1)} %broadcast_select_fusion.3), channel_id=1, source_target_pairs={{64,0},{80,16},{96,32},{112,48},{128,64},{144,80},{160,96},{176,11... | collective-permute-start | bytes 663560 | tf_op jit(solution)/shard_map/ppermute | solution.py:15
  48.6 15.6 %collective-permute-start.8 = (bf16[1,48,2304]{2,1,0:T(8,128)(2,1)S(1)}, bf16[1,48,2304]{2,1,0:T(8,128)(2,1)S(1)}, u32[]{:S(2)}, u32[]{:S(2)}) collective-permute-start(bf16[1,48,2304]{2,1,0:T(8,128)(2,1)S(1)} %broadcast_select_fusion.4), channel_id=1, source_target_pairs={{384,0},{400,16},{416,32},{432,48},{448,64},{464,80},{480,96},{496... | collective-permute-start | bytes 663560 | tf_op jit(solution)/shard_map/ppermute | solution.py:15
  52.4 14.2 %collective-permute-start.3 = (bf16[1,48,2304]{2,1,0:T(8,128)(2,1)S(1)}, bf16[1,48,2304]{2,1,0:T(8,128)(2,1)S(1)}, u32[]{:S(2)}, u32[]{:S(2)}) collective-permute-start(bf16[1,48,2304]{2,1,0:T(8,128)(2,1)S(1)} %broadcast_select_fusion.5), channel_id=1, source_target_pairs={{128,0},{144,16},{160,32},{176,48},{192,64},{208,80},{224,96},{240... | collective-permute-start | bytes 663560 | tf_op jit(solution)/shard_map/ppermute | solution.py:15
  64.3 24.0 %copy-start = (bf16[1,48,2304]{2,1,0:T(8,128)(2,1)}, bf16[1,48,2304]{2,1,0:T(8,128)(2,1)S(1)}, u32[]{:S(2)}) copy-start(bf16[1,48,2304]{2,1,0:T(8,128)(2,1)S(1)} %broadcast_select_fusion.6) | copy-start | bytes 663556
  64.3 18.3 %collective-permute-start.9 = (bf16[1,48,2304]{2,1,0:T(8,128)(2,1)S(1)}, bf16[1,48,2304]{2,1,0:T(8,128)(2,1)S(1)}, u32[]{:S(2)}, u32[]{:S(2)}) collective-permute-start(bf16[1,48,2304]{2,1,0:T(8,128)(2,1)S(1)} %broadcast_select_fusion.6), channel_id=1, source_target_pairs={{256,0},{272,16},{288,32},{304,48},{320,64},{336,80},{352,96},{368... | collective-permute-start | bytes 663560 | tf_op jit(solution)/shard_map/ppermute | solution.py:15
  66.7 21.5 %copy-start.2 = (bf16[1,48,2304]{2,1,0:T(8,128)(2,1)}, bf16[1,48,2304]{2,1,0:T(8,128)(2,1)S(1)}, u32[]{:S(2)}) copy-start(bf16[1,48,2304]{2,1,0:T(8,128)(2,1)S(1)} %broadcast_select_fusion.7) | copy-start | bytes 663556
  66.7 20.6 %collective-permute-start.4 = (bf16[1,48,2304]{2,1,0:T(8,128)(2,1)S(1)}, bf16[1,48,2304]{2,1,0:T(8,128)(2,1)S(1)}, u32[]{:S(2)}, u32[]{:S(2)}) collective-permute-start(bf16[1,48,2304]{2,1,0:T(8,128)(2,1)S(1)} %broadcast_select_fusion.7), channel_id=1, source_target_pairs={{256,0},{272,16},{288,32},{304,48},{320,64},{336,80},{352,96},{368... | collective-permute-start | bytes 663560 | tf_op jit(solution)/shard_map/ppermute | solution.py:15
  73.6 15.4 %copy-start.15 = (f32[48,1,25]{0,2,1:T(8,128)}, f32[48,1,25]{0,2,1:T(8,128)S(1)}, u32[]{:S(2)}) copy-start(f32[48,1,25]{0,2,1:T(8,128)S(1)} %get-tuple-element.70) | copy-start | bytes 14404
  73.6 15.4 %copy-start.17 = (f32[48,1,25]{0,2,1:T(8,128)}, f32[48,1,25]{0,2,1:T(8,128)S(1)}, u32[]{:S(2)}) copy-start(f32[48,1,25]{0,2,1:T(8,128)S(1)} %get-tuple-element.71) | copy-start | bytes 14404
  82.6 5.7 %copy-start.11 = (bf16[1,48,2304]{2,1,0:T(8,128)(2,1)}, bf16[1,48,2304]{2,1,0:T(8,128)(2,1)S(1)}, u32[]{:S(2)}) copy-start(bf16[1,48,2304]{2,1,0:T(8,128)(2,1)S(1)} %collective-permute-done.9) | copy-start | bytes 663556
  87.3 0.9 copy-start.13
  98.2 1.2 copy-start.7
  105.7 3.0 %copy-start.16 = (f32[48,1,25]{0,2,1:T(8,128)S(1)}, f32[48,1,25]{0,2,1:T(8,128)}, u32[]{:S(2)}) copy-start(f32[48,1,25]{0,2,1:T(8,128)} %copy-done.15) | copy-start | bytes 14404
  105.7 3.0 %copy-start.18 = (f32[48,1,25]{0,2,1:T(8,128)S(1)}, f32[48,1,25]{0,2,1:T(8,128)}, u32[]{:S(2)}) copy-start(f32[48,1,25]{0,2,1:T(8,128)} %copy-done.17) | copy-start | bytes 14404
  115.7 2.2 %copy-start.10 = (f32[2,48,2,48]{1,3,2,0:T(8,128)S(1)}, f32[2,48,2,48]{1,3,2,0:T(8,128)}, u32[]{:S(2)}) copy-start(f32[2,48,2,48]{1,3,2,0:T(8,128)} %copy-done.9) | copy-start | bytes 110596
  117.9 1.2 copy-start.8
  125.5 0.9 copy-start.1
  125.5 1.0 copy-start.3
  125.5 1.1 copy-start.5
  125.5 1.3 copy-start.6
  125.5 1.4 copy-start.12
  125.5 1.4 copy-start.14
where the time goes:
time: 165 us
  starting transfers between devices  43.6 us (26%)
  waiting for transfers between devices  41.7 us (25%)
  blocking collectives  36.1 us (22%)
  matrix products  30.6 us (19%)
  local copies, waits for them, and re-layouts  8.98 us (5%)
  other arithmetic  3.15 us (2%)
    ppermute x10, starting transfers between devices, from_behind(): return lax.ppermute(block, axis, route)  43.6 us
    ppermute x10, waiting for transfers between devices, from_behind(): return lax.ppermute(block, axis, route)  41.7 us
    all_to_all x1, blocking collectives, summed_on_arrival(): lax.all_to_all(blocks, axis, split_axis=0, concat_axis=0, tiled=True)  36.1 us
    dot_general x12, matrix products, contract(): return jnp.einsum(form, data, table, precision=lax.Precision.HIGHEST)  30.6 us
  transfers between devices with their start and end apart: 10, of which 9 were waited for; matrix products, arithmetic and copies ran while one was open for 1% of the time, Pallas kernels for 0%

commit v1 on v0

v1 whole, which is shorter than its diff:
```python
import math

import jax
import jax.numpy as jnp
import numpy as np
from jax import lax
from jax.experimental import pallas as pl
from jax.experimental.pallas import tpu as pltpu
from jax.sharding import PartitionSpec as P

MESH = pl.DeviceIdType.MESH
F32 = jnp.float32
BF16 = jnp.bfloat16

cell_edge = 59.0
screen_rate = 0.106

NG = 48
CELLS = NG * NG
HALF = 64
ROWS = 12
SLAB = 72


def tables():
    n = np.arange(NG)
    basis = np.zeros((NG, NG))
    basis[0] = 1.0 / math.sqrt(NG)
    for k in range(1, NG // 2):
        basis[k] = math.sqrt(2.0 / NG) * np.cos(2.0 * math.pi * ((k * n) % NG) / NG)
        basis[NG // 2 + k] = math.sqrt(2.0 / NG) * np.sin(2.0 * math.pi * ((k * n) % NG) / NG)
    basis[NG // 2] = np.cos(math.pi * n) / math.sqrt(NG)
    high = basis.astype(jnp.bfloat16).astype(np.float64)
    low = (basis - high).astype(jnp.bfloat16).astype(np.float64)

    def right(h, l):
        table = np.zeros((256, 256))
        for p in range(2):
            at = slice(p * HALF, p * HALF + NG)
            table[at, at] = h
            table[at, 128 + p * HALF : 128 + p * HALF + NG] = l
            table[128 + p * HALF : 128 + p * HALF + NG, at] = h
        return table

    def left(h, l):
        table = np.zeros((NG, 256))
        table[:, : 3 * NG] = np.concatenate([h, h, l], axis=1)
        return table

    whole = [right(high.T, low.T), right(high, low), left(high, low), left(high.T, low.T)]
    return np.concatenate(whole, axis=0).astype(jnp.bfloat16)


def halves(v):
    high = v.astype(BF16)
    low = (v - high.astype(F32)).astype(BF16)
    return high, low


def dot(a, b):
    return jnp.dot(a, b, preferred_element_type=F32)


def along_lanes(v, table):
    high, low = halves(v)
    both = dot(jnp.concatenate([high, low], axis=1), table)
    return both[:, :128] + both[:, 128:]


def along_rows(v, table):
    high, low = halves(v)
    return dot(table, jnp.concatenate([high, low, high], axis=0))


def to_lanes(v, count):
    return jnp.concatenate([v[i * NG : (i + 1) * NG] for i in range(count)], axis=1)


def to_rows(v, count):
    return jnp.concatenate([v[:, i * 128 : (i + 1) * 128] for i in range(count)], axis=0)


def spread_table(offset, depth, which):
    row = lax.broadcasted_iota(jnp.int32, (depth, 256), 0)
    lane = lax.broadcasted_iota(jnp.int32, (depth, 256), 1)
    cell = lane % HALF
    wanted = offset + NG * (lane // 128) + cell
    hit = (row == wanted) & (cell < NG)
    if which is not None:
        hit = hit & ((lane // HALF) % 2 == which)
    return jnp.where(hit, 1.0, 0.0).astype(BF16)


WINDOWS = ((0, 128, 0), (0, 256, 96), (128, 256, 64), (256, 128, 32))


def spread(parts, out_ref):
    for pair, (first, depth, offset) in enumerate(WINDOWS):
        total = None
        for ref, which in parts:
            rows = jnp.concatenate(
                [ref[:, g * 384 + first : g * 384 + first + depth] for g in range(6)], axis=0
            )
            term = dot(rows, spread_table(offset, depth, which))
            total = term if total is None else total + term
        for g in range(6):
            for side in range(2):
                y = g * 8 + pair * 2 + side
                out_ref[pl.ds(y, NG, stride=NG), :] = total[
                    g * NG : (g + 1) * NG, side * 128 : (side + 1) * 128
                ]


def signed_square(k):
    m = jnp.where(k > NG // 2, k - NG // 2, k)
    return m * m


def fill_kernel(kernel_ref):
    row = lax.broadcasted_iota(jnp.int32, (NG, 128), 0)
    lane = lax.broadcasted_iota(jnp.int32, (NG, 128), 1) % HALF
    plane = signed_square(row) + signed_square(lane)

    def one(k, carry):
        squared = plane + signed_square(k)
        wave_sq = squared.astype(F32) * F32((2.0 * math.pi / cell_edge) ** 2)
        safe_sq = jnp.where(squared == 0, F32(1.0), wave_sq)
        damped = F32(1.0) - jnp.exp(-safe_sq * F32(1.0 / (4.0 * screen_rate**2)))
        screened = F32(4.0 * math.pi) * damped / safe_sq
        value = jnp.where(squared == 0, F32(math.pi / screen_rate**2), screened)
        kernel_ref[pl.ds(pl.multiple_of(k * NG, NG), NG), :] = value
        return carry

    lax.fori_loop(0, NG, one, 0)


def exchange_kernel(
    own_ref, table_ref, out_ref,
    partner, own_wide, partner_wide, field, kernel, partial,
    from_core, chip_sum, from_x, row_sum, from_y,
    in_send, in_recv, core_send, core_recv, x_send, x_recv, y_send, y_recv,
):
    blk = lax.axis_index("blk")
    off = lax.axis_index("off")
    z, y_lo = blk // 4, blk % 4
    x, y_hi, core = off // 4, (off // 2) % 2, off % 2
    y = y_hi * 4 + y_lo

    def device(x, y, z, core):
        y = lax.rem(y + 8, 8)
        z = lax.rem(z + 8, 8)
        return (z * 4 + lax.rem(y, 4), (x * 2 + y // 4) * 2 + core)

    dy = lax.rem(x + 1, 4) - 1

    def dz_of(y_hi, k):
        even = jnp.where(core == 0, -2 * k, 2 + 2 * k)
        odd = jnp.where(core == 0, 1 - 4 * k, -1 + 4 * k)
        return jnp.where(y_hi == 0, even, odd)

    sources, targets = [], []
    for k in range(2):
        sources.append(device(x, y + dy, z + dz_of(y_hi, k), core))
        ty = lax.rem(y - dy + 8, 8)
        targets.append(device(x, ty, z - dz_of(ty // 4, k), core))
    itself = (x == 0) & (y_hi == 0) & (core == 0)

    sibling = (blk, (x * 2 + y_hi) * 2 + 1 - core)
    opposite = (blk, (x * 2 + 1 - y_hi) * 2 + core)

    def at_x(cx):
        return (blk, (cx * 2 + y_hi) * 2 + core)

    barrier = pltpu.get_barrier_semaphore()

    def greet(device_id):
        pl.semaphore_signal(barrier, inc=1, device_id=device_id, device_id_type=MESH)

    @pl.when(jnp.logical_not(itself))
    def _():
        greet(sources[0])

    greet(sources[1])
    greet(sibling)
    greet(opposite)
    for s in range(3):
        greet(at_x(lax.rem(x + 1 + s, 4)))

    @pl.when(itself)
    def _():
        pl.semaphore_wait(barrier, 6)

    @pl.when(jnp.logical_not(itself))
    def _():
        pl.semaphore_wait(barrier, 7)

    inputs = [
        pltpu.make_async_remote_copy(
            src_ref=own_ref,
            dst_ref=partner.at[k],
            send_sem=in_send.at[k],
            recv_sem=in_recv.at[k],
            device_id=targets[k],
            device_id_type=MESH,
        )
        for k in range(2)
    ]

    inputs[1].start()

    @pl.when(jnp.logical_not(itself))
    def _():
        inputs[0].start()

    spread([(own_ref, None)], own_wide)
    fill_kernel(kernel)

    @pl.when(itself)
    def _():
        partner[0] = own_ref[...]

    @pl.when(jnp.logical_not(itself))
    def _():
        inputs[0].wait()

    inputs[1].wait()

    spread([(partner.at[0], 0), (partner.at[1], 1)], partner_wide)

    right_forward = table_ref.at[pl.ds(0, 256)]
    right_backward = table_ref.at[pl.ds(256, 256)]
    left_forward = table_ref.at[pl.ds(512, NG), pl.ds(0, 3 * NG)]
    left_backward = table_ref.at[pl.ds(512 + NG, NG), pl.ds(0, 3 * NG)]

    def forward(i, carry):
        at = pl.ds(pl.multiple_of(i * (ROWS * NG), ROWS * NG), ROWS * NG)
        density = own_wide[at, :] * partner_wide[at, :]
        wide = to_lanes(along_lanes(density, right_forward[...]), ROWS)
        field[at, :] = to_rows(along_rows(wide, left_forward[...]), ROWS)
        return carry

    lax.fori_loop(0, NG // ROWS, forward, 0)

    def middle(i, carry):
        columns = [
            field[pl.ds(i * ROWS + j, NG, stride=NG), :] for j in range(ROWS)
        ]
        spectrum = along_rows(jnp.concatenate(columns, axis=1), left_forward[...])
        at = pl.ds(pl.multiple_of(i * (ROWS * NG), ROWS * NG), ROWS * NG)
        spectrum = spectrum * to_lanes(kernel[at, :], ROWS)
        back = along_rows(spectrum, left_backward[...])
        for j in range(ROWS):
            field[pl.ds(i * ROWS + j, NG, stride=NG), :] = back[:, j * 128 : (j + 1) * 128]
        return carry

    lax.fori_loop(0, NG // ROWS, middle, 0)

    low_half = lax.broadcasted_iota(jnp.int32, (NG // 2, 128), 1) < HALF

    core_copies, x_copies = [], []
    for s in range(4):
        cx = lax.rem(x + 1 + s, 4)
        core_copies.append(
            pltpu.make_async_remote_copy(
                src_ref=partial.at[cx, :, 1 - core],
                dst_ref=from_core.at[s],
                send_sem=core_send.at[s],
                recv_sem=core_recv.at[s],
                device_id=sibling,
                device_id_type=MESH,
            )
        )
        if s < 3:
            x_copies.append(
                pltpu.make_async_remote_copy(
                    src_ref=chip_sum.at[s],
                    dst_ref=from_x.at[s],
                    send_sem=x_send.at[s],
                    recv_sem=x_recv.at[s],
                    device_id=at_x(cx),
                    device_id_type=MESH,
                )
            )

    def sum_cores(s):
        cx = lax.rem(x + 1 + s, 4)
        core_copies[s].wait()
        for h in range(2):
            chip_sum[s, h] = partial[cx, h, core] + from_core[s, h]
        if s < 3:
            x_copies[s].start()

    for s in range(4):
        cx = lax.rem(x + 1 + s, 4)
        at = pl.ds(pl.multiple_of(cx * (ROWS * NG), ROWS * NG), ROWS * NG)
        wide = along_rows(to_lanes(field[at, :], ROWS), left_backward[...])
        potential = along_lanes(to_rows(wide, ROWS), right_backward[...])
        terms = potential * partner_wide[at, :]
        for i in range(ROWS):
            a = terms[i * NG : i * NG + NG // 2]
            b = terms[i * NG + NG // 2 : (i + 1) * NG]
            swapped = pltpu.roll(jnp.where(low_half, b, a), HALF, 1)
            row = jnp.where(low_half, a, b) + swapped
            partial[cx, i // 6, (i // 3) % 2, pl.ds((i % 3) * 24, 24), :] = row
        core_copies[s].start()
        if s > 0:
            sum_cores(s - 1)
    sum_cores(3)

    for c in x_copies:
        c.wait()
    for h in range(2):
        row_sum[h] = (chip_sum[3, h] + from_x[0, h]) + (from_x[1, h] + from_x[2, h])

    last = pltpu.make_async_remote_copy(
        src_ref=row_sum.at[1 - y_hi],
        dst_ref=from_y,
        send_sem=y_send,
        recv_sem=y_recv,
        device_id=opposite,
        device_id_type=MESH,
    )
    last.start()
    last.wait()
    out_ref[...] = F32(-0.25) * (row_sum[y_hi] + from_y[...])


def on_device(orbitals):
    vmem = pl.BlockSpec(memory_space=pltpu.VMEM)
    wide = pltpu.VMEM((CELLS, 128), F32)
    dma = pltpu.SemaphoreType.DMA
    found = pl.pallas_call(
        exchange_kernel,
        out_shape=jax.ShapeDtypeStruct((SLAB, 128), F32),
        in_specs=[vmem, vmem],
        out_specs=vmem,
        scratch_shapes=[
            pltpu.VMEM((2, NG, CELLS), BF16),
            wide, wide, wide, wide,
            pltpu.VMEM((4, 2, 2, SLAB, 128), F32),
            pltpu.VMEM((4, 2, SLAB, 128), F32),
            pltpu.VMEM((4, 2, SLAB, 128), F32),
            pltpu.VMEM((3, 2, SLAB, 128), F32),
            pltpu.VMEM((2, SLAB, 128), F32),
            pltpu.VMEM((SLAB, 128), F32),
            dma((2,)), dma((2,)), dma((4,)), dma((4,)),
            dma((3,)), dma((3,)), dma, dma,
        ],
        compiler_params=pltpu.CompilerParams(
            collective_id=0, has_side_effects=True, vmem_limit_bytes=48 * 2**20
        ),
    )(orbitals[0], jnp.asarray(tables()))
    cells = found.reshape(3, 24, 2, HALF).transpose(0, 2, 1, 3)[..., :NG]
    return cells.reshape(1, 3, CELLS)


def solution(mesh):
    return jax.shard_map(
        on_device,
        mesh=mesh,
        in_specs=(P("blk", None, None),),
        out_specs=P("blk", "off", None),
        check_vma=False,
    )
```

time: 165 us -> 56.1 us (0.34)
  the two profiles are of different devices: /device:TPU:9 before, /device:TPU:1 now
where the time goes in v1:
time: 56.1 us; the launch traced here: 55.9 us
  Pallas kernels  53.1 us (95%)
  local copies, waits for them, and re-layouts  2.74 us (5%)
    pallas_call x1, Pallas kernels, on_device(): pl.pallas_call(exchange_kernel, out_shape=jax.ShapeDtypeStruct((SLAB, 128...  53.1 us
    unnamed x4, local copies, waits for them, and re-layouts  1.9 us

profile of v1, /device:TPU:1, one launch (start us, length us, event | category | flops | bytes accessed | tf_op | source)
XLA Modules:
  0.0 55.9 jit_solution(9921018506710529081)
XLA Ops:
  0.0 0.0 copy-start
  0.0 1.0 %copy-done = bf16[608,256]{1,0:T(8,128)(2,1)S(1)} copy-done((bf16[608,256]{1,0:T(8,128)(2,1)S(1)}, bf16[608,256]{1,0:T(8,128)(2,1)}, u32[]{:S(2)}) %copy-start) | copy-done | bytes 311320
  1.0 0.0 copy-start.1
  1.0 0.9 %copy-done.1 = bf16[1,48,2304]{2,1,0:T(8,128)(2,1)S(1)} copy-done((bf16[1,48,2304]{2,1,0:T(8,128)(2,1)S(1)}, bf16[1,48,2304]{2,1,0:T(8,128)(2,1)}, u32[]{:S(2)}) %copy-start.1) | copy-done | bytes 221208
  1.9 53.1 %shard_map.28 = f32[72,128]{1,0:T(8,128)S(1)} custom-call(bf16[48,2304]{1,0:T(8,128)(2,1)S(1)} %bitcast.5, bf16[608,256]{1,0:T(8,128)(2,1)S(1)} %copy-done), custom_call_target="tpu_custom_call" | custom-call | tf_op jit(solution)/shard_map/pallas_call | solution.py:332
  55.1 0.1 reshape.6
  55.2 0.7 %reshape.7 = f32[1,3,2304]{2,0,1:T(1,128)} reshape(f32[3,2,24,48]{3,2,1,0:T(8,128)S(1)} %copy.3) | data formatting | bytes 55296 | tf_op jit(solution)/shard_map/reshape | solution.py:354
  (1 shorter events, 0.0 us)
Async XLA Ops:
  0.0 1.0 %copy-start = (bf16[608,256]{1,0:T(8,128)(2,1)S(1)}, bf16[608,256]{1,0:T(8,128)(2,1)}, u32[]{:S(2)}) copy-start(bf16[608,256]{1,0:T(8,128)(2,1)} %constant.2.clone.table_ref) | copy-start | bytes 933892
  1.0 0.9 %copy-start.1 = (bf16[1,48,2304]{2,1,0:T(8,128)(2,1)S(1)}, bf16[1,48,2304]{2,1,0:T(8,128)(2,1)}, u32[]{:S(2)}) copy-start(bf16[1,48,2304]{2,1,0:T(8,128)(2,1)} %param.2) | copy-start | bytes 663556

commit v2 on v1

v2 whole, which is shorter than its diff:
```python
import math

import jax
import jax.numpy as jnp
import numpy as np
from jax import lax
from jax.experimental import pallas as pl
from jax.experimental.pallas import tpu as pltpu
from jax.sharding import PartitionSpec as P

MESH = pl.DeviceIdType.MESH
F32 = jnp.float32
BF16 = jnp.bfloat16

cell_edge = 59.0
screen_rate = 0.106

NG = 48
CELLS = NG * NG
HALF = 64
ROWS = 12
SLAB = 72
PACKED = 56
CHUNKS = 3
CHUNK = NG // CHUNKS


def tables():
    n = np.arange(NG)
    basis = np.zeros((NG, NG))
    basis[0] = 1.0 / math.sqrt(NG)
    for k in range(1, NG // 2):
        basis[k] = math.sqrt(2.0 / NG) * np.cos(2.0 * math.pi * ((k * n) % NG) / NG)
        basis[NG // 2 + k] = math.sqrt(2.0 / NG) * np.sin(2.0 * math.pi * ((k * n) % NG) / NG)
    basis[NG // 2] = np.cos(math.pi * n) / math.sqrt(NG)
    high = basis.astype(jnp.bfloat16).astype(np.float64)
    low = (basis - high).astype(jnp.bfloat16).astype(np.float64)

    def right(h, l):
        table = np.zeros((256, 256))
        for p in range(2):
            at = slice(p * HALF, p * HALF + NG)
            table[at, at] = h
            table[at, 128 + p * HALF : 128 + p * HALF + NG] = l
            table[128 + p * HALF : 128 + p * HALF + NG, at] = h
        return table

    def left(h, l):
        table = np.zeros((NG, 256))
        table[:, : 3 * NG] = np.concatenate([h, h, l], axis=1)
        return table

    whole = [right(high.T, low.T), right(high, low), left(high, low), left(high.T, low.T)]
    return np.concatenate(whole, axis=0).astype(jnp.bfloat16)


def halves(v):
    high = v.astype(BF16)
    low = (v - high.astype(F32)).astype(BF16)
    return high, low


def dot(a, b):
    return jnp.dot(a, b, preferred_element_type=F32)


def along_lanes(v, table):
    high, low = halves(v)
    both = dot(jnp.concatenate([high, low], axis=1), table)
    return both[:, :128] + both[:, 128:]


def along_rows(v, table):
    high, low = halves(v)
    return dot(table, jnp.concatenate([high, low, high], axis=0))


def to_lanes(v, count):
    return jnp.concatenate([v[i * NG : (i + 1) * NG] for i in range(count)], axis=1)


def to_rows(v, count):
    return jnp.concatenate([v[:, i * 128 : (i + 1) * 128] for i in range(count)], axis=0)


WINDOWS = ((0, 128, 0), (0, 256, 96), (128, 256, 64), (256, 128, 32))
STARTS = (0, 128, 384, 640)
SPREAD = 768


def fill_spread(spread_ref):
    for (_, depth, offset), start in zip(WINDOWS, STARTS):
        row = lax.broadcasted_iota(jnp.int32, (depth, 256), 0)
        lane = lax.broadcasted_iota(jnp.int32, (depth, 256), 1)
        cell = lane % HALF
        hit = (row == offset + NG * (lane // 128) + cell) & (cell < NG)
        second = (lane // HALF) % 2 == 1
        for which, kept in enumerate((hit & ~second, hit & second, hit)):
            spread_ref[which, start : start + depth, :] = jnp.where(kept, 1.0, 0.0).astype(BF16)


def spread(parts, spread_ref, out_ref, start, count):
    for pair, (first, depth, _) in enumerate(WINDOWS):
        total = None
        for ref, which in parts:
            rows = jnp.concatenate(
                [
                    ref[start : start + count, g * 384 + first : g * 384 + first + depth]
                    for g in range(6)
                ],
                axis=0,
            )
            term = dot(rows, spread_ref[which, STARTS[pair] : STARTS[pair] + depth, :])
            total = term if total is None else total + term
        for g in range(6):
            for side in range(2):
                y = g * 8 + pair * 2 + side
                out_ref[pl.ds(start * NG + y, count, stride=NG), :] = total[
                    g * count : (g + 1) * count, side * 128 : (side + 1) * 128
                ]


def gap_lanes(rows):
    return lax.broadcasted_iota(jnp.int32, (rows, 128), 1) % HALF >= NG


def packed(slab):
    moved = [
        pltpu.roll(slab[56 + 8 * (q // 3) : 64 + 8 * (q // 3)], NG - 16 * (q % 3), 1)
        for q in range(6)
    ]
    filled = jnp.where(gap_lanes(48), jnp.concatenate(moved, axis=0), slab[:48])
    return jnp.concatenate([filled, slab[48:56]], axis=0)


def unpacked(slab):
    place = lax.broadcasted_iota(jnp.int32, (8, 128), 1) % HALF // 16
    tiles = [slab]
    for v in range(2):
        tile = jnp.zeros((8, 128), F32)
        for q in range(3):
            piece = slab[(v * 3 + q) * 8 : (v * 3 + q) * 8 + 8]
            tile = jnp.where(place == q, pltpu.roll(piece, 80 + 16 * q, 1), tile)
        tiles.append(tile)
    return jnp.concatenate(tiles, axis=0)


def signed_square(k):
    m = jnp.where(k > NG // 2, k - NG // 2, k)
    return m * m


def fill_kernel(kernel_ref):
    row = lax.broadcasted_iota(jnp.int32, (NG, 128), 0)
    lane = lax.broadcasted_iota(jnp.int32, (NG, 128), 1) % HALF
    plane = signed_square(row) + signed_square(lane)

    def one(k, carry):
        squared = plane + signed_square(k)
        wave_sq = squared.astype(F32) * F32((2.0 * math.pi / cell_edge) ** 2)
        safe_sq = jnp.where(squared == 0, F32(1.0), wave_sq)
        damped = F32(1.0) - jnp.exp(-safe_sq * F32(1.0 / (4.0 * screen_rate**2)))
        screened = F32(4.0 * math.pi) * damped / safe_sq
        value = jnp.where(squared == 0, F32(math.pi / screen_rate**2), screened)
        kernel_ref[pl.ds(pl.multiple_of(k * NG, NG), NG), :] = value
        return carry

    lax.fori_loop(0, NG, one, 0)


def pick(index, values):
    result = values[-1]
    for i in range(len(values) - 1):
        result = jnp.where(index == i, values[i], result)
    return result


def exchange_kernel(
    own_ref, table_ref, out_ref,
    own, table, spread_ref, partner, own_wide, partner_wide, field, kernel,
    partial, from_x, row_sum, from_y,
    copy_sem, in_send, in_recv, x_send, x_recv, y_send, y_recv,
):
    blk = lax.axis_index("blk")
    off = lax.axis_index("off")
    z, y_lo = blk // 4, blk % 4
    x, y_hi, core = off // 4, (off // 2) % 2, off % 2
    y = y_hi * 4 + y_lo

    load_own = pltpu.make_async_copy(own_ref, own, copy_sem.at[0])
    load_table = pltpu.make_async_copy(table_ref, table, copy_sem.at[1])
    load_own.start()
    load_table.start()

    def device(x, y, z, core):
        y = lax.rem(y + 8, 8)
        z = lax.rem(z + 8, 8)
        return (z * 4 + lax.rem(y, 4), (x * 2 + y // 4) * 2 + core)

    sources, targets = [], []
    for k in range(2):
        dy = pick(lax.rem(core * 2 + k + x, 4), (0, 1, 2 - 4 * lax.rem(x, 2), -1))

        def dz_of(y_hi):
            even = jnp.where(core == 0, 4 * k, 2 - 4 * k)
            odd = jnp.where(core == 0, 1 - 4 * k, 3 - 4 * k)
            return jnp.where(y_hi == 0, even, odd)

        sources.append(device(x, y + dy, z + dz_of(y_hi), core))
        ty = lax.rem(y - dy + 8, 8)
        targets.append(device(x, ty, z - dz_of(ty // 4), core))
    itself = (x == 0) & (y_hi == 0) & (core == 0)
    opposite = (blk, (x * 2 + 1 - y_hi) * 2 + core)

    def neighbour(ahead, other):
        cx = lax.rem(x + ahead, 4)
        return (blk, (cx * 2 + y_hi) * 2 + (1 - core if other else core))

    around = [(ahead, other) for ahead in (1, 2, 3, 0) for other in range(2) if ahead or other]

    barrier = pltpu.get_barrier_semaphore()

    def greet(device_id):
        pl.semaphore_signal(barrier, inc=1, device_id=device_id, device_id_type=MESH)

    greet(opposite)
    greet(sources[1])

    @pl.when(jnp.logical_not(itself))
    def _():
        greet(sources[0])

    for ahead, other in around:
        greet(neighbour(ahead, other))

    @pl.when(itself)
    def _():
        pl.semaphore_wait(barrier, 9)

    @pl.when(jnp.logical_not(itself))
    def _():
        pl.semaphore_wait(barrier, 10)

    def arrival(k, c):
        at = pl.ds(c * CHUNK, CHUNK)
        return pltpu.make_async_remote_copy(
            src_ref=own_ref.at[at],
            dst_ref=partner.at[k, at],
            send_sem=in_send.at[k, c],
            recv_sem=in_recv.at[k, c],
            device_id=targets[k],
            device_id_type=MESH,
        )

    for c in range(CHUNKS):
        arrival(1, c).start()

        @pl.when(jnp.logical_not(itself))
        def _():
            arrival(0, c).start()

    fill_spread(spread_ref)
    load_own.wait()
    spread([(own, 2)], spread_ref, own_wide, 0, NG)
    fill_kernel(kernel)
    load_table.wait()

    right_forward = table.at[pl.ds(0, 256)]
    right_backward = table.at[pl.ds(256, 256)]
    left_forward = table.at[pl.ds(512, NG), pl.ds(0, 3 * NG)]
    left_backward = table.at[pl.ds(512 + NG, NG), pl.ds(0, 3 * NG)]

    @pl.when(itself)
    def _():
        partner[0] = own[...]

    for c in range(CHUNKS):

        @pl.when(jnp.logical_not(itself))
        def _():
            arrival(0, c).wait()

        arrival(1, c).wait()
        spread([(partner.at[0], 0), (partner.at[1], 1)], spread_ref, partner_wide, c * CHUNK, CHUNK)
        at = pl.ds(c * CHUNK * NG, CHUNK * NG)
        density = own_wide[at, :] * partner_wide[at, :]
        wide = to_lanes(along_lanes(density, right_forward[...]), CHUNK)
        field[at, :] = to_rows(along_rows(wide, left_forward[...]), CHUNK)

    def middle(i, carry):
        columns = [field[pl.ds(i * ROWS + j, NG, stride=NG), :] for j in range(ROWS)]
        spectrum = along_rows(jnp.concatenate(columns, axis=1), left_forward[...])
        at = pl.ds(pl.multiple_of(i * (ROWS * NG), ROWS * NG), ROWS * NG)
        spectrum = spectrum * to_lanes(kernel[at, :], ROWS)
        back = along_rows(spectrum, left_backward[...])
        for j in range(ROWS):
            field[pl.ds(i * ROWS + j, NG, stride=NG), :] = back[:, j * 128 : (j + 1) * 128]
        return carry

    lax.fori_loop(0, NG // ROWS, middle, 0)

    def departure(h, ahead, other):
        return pltpu.make_async_remote_copy(
            src_ref=partial.at[h, ahead, other],
            dst_ref=from_x.at[h, (4 - ahead) % 4, other],
            send_sem=x_send.at[h, ahead, other],
            recv_sem=x_recv.at[h, (4 - ahead) % 4, other],
            device_id=neighbour(ahead, other),
            device_id_type=MESH,
        )

    low_half = lax.broadcasted_iota(jnp.int32, (NG // 2, 128), 1) < HALF

    for h in range(2):
        kept_hi = 1 - y_hi if h == 0 else y_hi
        for pair in ((1, 2), (3, 0)):
            starts = [
                pl.multiple_of((lax.rem(x + ahead, 4) * 2 + kept_hi) * (6 * NG), 6 * NG)
                for ahead in pair
            ]
            spectrum = jnp.concatenate([field[pl.ds(at, 6 * NG), :] for at in starts], axis=0)
            wide = along_rows(to_lanes(spectrum, 12), left_backward[...])
            potential = along_lanes(to_rows(wide, 12), right_backward[...])
            for n, (ahead, at) in enumerate(zip(pair, starts)):
                terms = potential[n * 6 * NG : (n + 1) * 6 * NG] * partner_wide[pl.ds(at, 6 * NG), :]
                for side in range(2):
                    planes = []
                    for i in range(side * 3, side * 3 + 3):
                        a = terms[i * NG : i * NG + NG // 2]
                        b = terms[i * NG + NG // 2 : (i + 1) * NG]
                        swapped = pltpu.roll(jnp.where(low_half, b, a), HALF, 1)
                        planes.append(jnp.where(low_half, a, b) + swapped)
                    other = jnp.where(core == side, 0, 1)
                    partial[h, ahead, other] = packed(jnp.concatenate(planes, axis=0))
                for other in range(2):
                    if ahead or other:
                        departure(h, ahead, other).start()

    def gathered(h):
        total = partial[h, 0, 0]
        for ahead, other in around:
            departure(h, ahead, other).wait()
        for ahead, other in around:
            total = total + from_x[h, ahead, other]
        return total

    row_sum[...] = gathered(0)
    last = pltpu.make_async_remote_copy(
        src_ref=row_sum,
        dst_ref=from_y,
        send_sem=y_send,
        recv_sem=y_recv,
        device_id=opposite,
        device_id_type=MESH,
    )
    last.start()
    kept = gathered(1)
    last.wait()
    out_ref[...] = unpacked(F32(-0.25) * (kept + from_y[...]))


def on_device(orbitals):
    anywhere = pl.BlockSpec(memory_space=pl.ANY)
    wide = pltpu.VMEM((CELLS, 128), F32)
    slab = (PACKED, 128)
    dma = pltpu.SemaphoreType.DMA
    constants = jnp.asarray(tables())
    found = pl.pallas_call(
        exchange_kernel,
        out_shape=jax.ShapeDtypeStruct((SLAB, 128), F32),
        in_specs=[anywhere, anywhere],
        out_specs=pl.BlockSpec(memory_space=pltpu.VMEM),
        scratch_shapes=[
            pltpu.VMEM((NG, CELLS), BF16),
            pltpu.VMEM(constants.shape, BF16),
            pltpu.VMEM((3, SPREAD, 256), BF16),
            pltpu.VMEM((2, NG, CELLS), BF16),
            wide, wide, wide, wide,
            pltpu.VMEM((2, 4, 2, *slab), F32),
            pltpu.VMEM((2, 4, 2, *slab), F32),
            pltpu.VMEM(slab, F32),
            pltpu.VMEM(slab, F32),
            dma((2,)),
            dma((2, CHUNKS)), dma((2, CHUNKS)),
            dma((2, 4, 2)), dma((2, 4, 2)),
            dma, dma,
        ],
        compiler_params=pltpu.CompilerParams(
            collective_id=0, has_side_effects=True, vmem_limit_bytes=60 * 2**20
        ),
    )(orbitals[0], constants)
    cells = found.reshape(3, 24, 2, HALF).transpose(0, 2, 1, 3)[..., :NG]
    return cells.reshape(1, 3, CELLS)


def solution(mesh):
    return jax.shard_map(
        on_device,
        mesh=mesh,
        in_specs=(P("blk", None, None),),
        out_specs=P("blk", "off", None),
        check_vma=False,
    )
```

time: 56.1 us -> 44.4 us (0.79)
  the two profiles are of different devices: /device:TPU:1 before, /device:TPU:56 now
where the time goes in v2:
time: 44.4 us; the launch traced here: 44.2 us
  Pallas kernels  42.6 us (96%)
  local copies, waits for them, and re-layouts  1.6 us (4%)
    pallas_call x1, Pallas kernels, on_device(): pl.pallas_call(exchange_kernel, out_shape=jax.ShapeDtypeStruct((SLAB, 128...  42.6 us

profile of v2, /device:TPU:56, one launch (start us, length us, event | category | flops | bytes accessed | tf_op | source)
XLA Modules:
  0.0 44.2 jit_solution(7402817106241928291)
XLA Ops:
  0.0 42.6 %shard_map.28 = f32[72,128]{1,0:T(8,128)} custom-call(bf16[48,2304]{1,0:T(8,128)(2,1)} %bitcast.6, bf16[608,256]{1,0:T(8,128)(2,1)} %constant.2.clone.table_ref), custom_call_target="tpu_custom_call" | custom-call | tf_op jit(solution)/shard_map/pallas_call | solution.py:368
  42.6 0.9 %reshape.6 = f32[3,24,2,64]{3,2,1,0:T(2,128)S(1)} reshape(f32[72,128]{1,0:T(8,128)} %shard_map.28) | data formatting | bytes 73728 | tf_op jit(solution)/shard_map/reshape | solution.py:392
  43.5 0.7 %reshape.7 = f32[1,3,2304]{2,0,1:T(1,128)} reshape(f32[3,2,24,48]{3,2,1,0:T(8,128)S(1)} %copy.3) | data formatting | bytes 55296 | tf_op jit(solution)/shard_map/reshape | solution.py:393
  (1 shorter events, 0.0 us)

commit v3 on v2

--- a/solution.py
+++ b/solution.py
@@ -21,6 +21,7 @@
 ROWS = 12
 SLAB = 72
 PACKED = 56
+EARLY = 3
 CHUNKS = 3
 CHUNK = NG // CHUNKS
 
@@ -168,6 +169,21 @@
     lax.fori_loop(0, NG, one, 0)
 
 
+def join_rows(planes_ref, out_ref):
+    lane = lax.broadcasted_iota(jnp.int32, (3, 128), 1)
+    full = [None] * (CELLS // 128)
+    for y in range(NG):
+        row = planes_ref[pl.ds(y % 24, 3, stride=24), :]
+        tile, at = divmod(y * NG, 128)
+        row = pltpu.roll(row, (at - HALF * (y // 24)) % 128, 1)
+        full[tile] = row if at == 0 else jnp.where(lane < at, full[tile], row)
+        if at + NG > 128:
+            full[tile + 1] = row
+    for tile, row in enumerate(full):
+        for plane in range(3):
+            out_ref[plane, :, tile * 128 : (tile + 1) * 128] = row[plane : plane + 1]
+
+
 def pick(index, values):
     result = values[-1]
     for i in range(len(values) - 1):
@@ -179,7 +195,7 @@
     own_ref, table_ref, out_ref,
     own, table, spread_ref, partner, own_wide, partner_wide, field, kernel,
     partial, from_x, row_sum, from_y,
-    copy_sem, in_send, in_recv, x_send, x_recv, y_send, y_recv,
+    planes_ref, copy_sem, in_send, in_recv, x_send, x_recv, y_send, y_recv, opposite_sem, go_sem,
 ):
     blk = lax.axis_index("blk")
     off = lax.axis_index("off")
@@ -223,23 +239,41 @@
     def greet(device_id):
         pl.semaphore_signal(barrier, inc=1, device_id=device_id, device_id_type=MESH)
 
-    greet(opposite)
-    greet(sources[1])
-
-    @pl.when(jnp.logical_not(itself))
-    def _():
-        greet(sources[0])
-
+    below, above = device(x, y - 2, z, core), device(x, y + 2, z, core)
+    greet(below)
+    greet(above)
     for ahead, other in around:
         greet(neighbour(ahead, other))
 
-    @pl.when(itself)
-    def _():
-        pl.semaphore_wait(barrier, 9)
-
-    @pl.when(jnp.logical_not(itself))
-    def _():
-        pl.semaphore_wait(barrier, 10)
+    mine_early = z < EARLY
+    moves = (jnp.logical_not(itself), itself | True)
+    to_early = [target[0] // 4 < EARLY for target in targets]
+    from_early = [source[0] // 4 < EARLY for source in sources]
+    defer_to = [moves[k] & mine_early & jnp.logical_not(to_early[k]) for k in range(2)]
+    defer_from = [moves[k] & jnp.logical_not(mine_early) & from_early[k] for k in range(2)]
+    greetings = 9
+    for k in range(2):
+
+        @pl.when(moves[k] & jnp.logical_not(defer_from[k]))
+        def _():
+            greet(sources[k])
+
+        @pl.when(defer_to[k])
+        def _():
+            greet(targets[k])
+
+        greetings = greetings + jnp.where(moves[k] & jnp.logical_not(defer_to[k]), 1, 0)
+        greetings = greetings + jnp.where(defer_from[k], 1, 0)
+
+    pl.semaphore_wait(barrier, greetings)
+
+    for k in range(2):
+
+        @pl.when(defer_from[k])
+        def _():
+            pl.semaphore_signal(
+                go_sem.at[k], inc=1, device_id=sources[k], device_id_type=MESH
+            )
 
     def arrival(k, c):
         at = pl.ds(c * CHUNK, CHUNK)
@@ -252,19 +286,39 @@
             device_id_type=MESH,
         )
 
+    later = [
+        moves[k] & jnp.logical_not(mine_early | to_early[k]) & to_early[1 - k]
+        for k in range(2)
+    ]
     for c in range(CHUNKS):
-        arrival(1, c).start()
-
-        @pl.when(jnp.logical_not(itself))
-        def _():
-            arrival(0, c).start()
-
+        for k in range(2):
+
+            @pl.when(moves[k] & jnp.logical_not(defer_to[k] | later[k]))
+            def _():
+                arrival(k, c).start()
+
+    pl.semaphore_signal(opposite_sem, inc=1, device_id=below, device_id_type=MESH)
     fill_spread(spread_ref)
     load_own.wait()
     spread([(own, 2)], spread_ref, own_wide, 0, NG)
     fill_kernel(kernel)
     load_table.wait()
 
+    for k in range(2):
+
+        @pl.when(defer_to[k])
+        def _():
+            pl.semaphore_wait(go_sem.at[k], 1)
+            for c in range(CHUNKS):
+                arrival(k, c).start()
+
+        @pl.when(later[k])
+        def _():
+            for c in range(CHUNKS):
+                arrival(1 - k, c).wait_send()
+            for c in range(CHUNKS):
+                arrival(k, c).start()
+
     right_forward = table.at[pl.ds(0, 256)]
     right_backward = table.at[pl.ds(256, 256)]
     left_forward = table.at[pl.ds(512, NG), pl.ds(0, 3 * NG)]
@@ -276,11 +330,11 @@
 
     for c in range(CHUNKS):
 
-        @pl.when(jnp.logical_not(itself))
-        def _():
-            arrival(0, c).wait()
-
-        arrival(1, c).wait()
+        @pl.when(moves[0])
+        def _():
+            arrival(0, c).wait_recv()
+
+        arrival(1, c).wait_recv()
         spread([(partner.at[0], 0), (partner.at[1], 1)], spread_ref, partner_wide, c * CHUNK, CHUNK)
         at = pl.ds(c * CHUNK * NG, CHUNK * NG)
         density = own_wide[at, :] * partner_wide[at, :]
@@ -345,6 +399,7 @@
         return total
 
     row_sum[...] = gathered(0)
+    pl.semaphore_wait(opposite_sem, 1)
     last = pltpu.make_async_remote_copy(
         src_ref=row_sum,
         dst_ref=from_y,
@@ -355,8 +410,17 @@
     )
     last.start()
     kept = gathered(1)
+
+    for k in range(2):
+
+        @pl.when(moves[k] & jnp.logical_not(later[1 - k]))
+        def _():
+            for c in range(CHUNKS):
+                arrival(k, c).wait_send()
+
     last.wait()
-    out_ref[...] = unpacked(F32(-0.25) * (kept + from_y[...]))
+    planes_ref[...] = unpacked(F32(-0.25) * (kept + from_y[...]))
+    join_rows(planes_ref, out_ref)
 
 
 def on_device(orbitals):
@@ -367,7 +431,7 @@
     constants = jnp.asarray(tables())
     found = pl.pallas_call(
         exchange_kernel,
-        out_shape=jax.ShapeDtypeStruct((SLAB, 128), F32),
+        out_shape=jax.ShapeDtypeStruct((3, 1, CELLS), F32),
         in_specs=[anywhere, anywhere],
         out_specs=pl.BlockSpec(memory_space=pltpu.VMEM),
         scratch_shapes=[
@@ -380,17 +444,19 @@
             pltpu.VMEM((2, 4, 2, *slab), F32),
             pltpu.VMEM(slab, F32),
             pltpu.VMEM(slab, F32),
+            pltpu.VMEM((SLAB, 128), F32),
             dma((2,)),
             dma((2, CHUNKS)), dma((2, CHUNKS)),
             dma((2, 4, 2)), dma((2, 4, 2)),
             dma, dma,
+            pltpu.SemaphoreType.REGULAR,
+            pltpu.SemaphoreType.REGULAR((2,)),
         ],
         compiler_params=pltpu.CompilerParams(
-            collective_id=0, has_side_effects=True, vmem_limit_bytes=60 * 2**20
+            collective_id=0, has_side_effects=True, vmem_limit_bytes=54 * 2**20 - 2**17
         ),
     )(orbitals[0], constants)
-    cells = found.reshape(3, 24, 2, HALF).transpose(0, 2, 1, 3)[..., :NG]
-    return cells.reshape(1, 3, CELLS)
+    return found.transpose(1, 0, 2)
 
 
 def solution(mesh):

time: 44.4 us -> 40.9 us (0.921)
  the two profiles are of different devices: /device:TPU:56 before, /device:TPU:1 now
where the time goes in v3:
time: 40.9 us; the launch traced here: 40.8 us
  Pallas kernels  40.2 us (98%)
  local copies, waits for them, and re-layouts  0.61 us (1%)
    pallas_call x1, Pallas kernels, on_device(): pl.pallas_call(exchange_kernel, out_shape=jax.ShapeDtypeStruct((3, 1, CEL...  40.2 us

profile of v3, /device:TPU:1, one launch (start us, length us, event | category | flops | bytes accessed | tf_op | source)
XLA Modules:
  0.0 40.8 jit_solution(4325844423163869923)
XLA Ops:
  0.0 40.2 %shard_map.28 = f32[3,1,2304]{2,1,0:T(1,128)S(1)} custom-call(bf16[48,2304]{1,0:T(8,128)(2,1)} %bitcast.3, bf16[608,256]{1,0:T(8,128)(2,1)} %constant.2.clone.table_ref), custom_call_target="tpu_custom_call" | custom-call | tf_op jit(solution)/shard_map/pallas_call | solution.py:432
  40.2 0.6 %copy.4 = f32[1,3,2304]{2,0,1:T(1,128)} copy(f32[1,3,2304]{2,0,1:T(1,128)S(1)} %bitcast.2) | data formatting | bytes 55296

commit v4 on v3

--- a/solution.py
+++ b/solution.py
@@ -18,10 +18,9 @@
 NG = 48
 CELLS = NG * NG
 HALF = 64
-ROWS = 12
 SLAB = 72
 PACKED = 56
-EARLY = 3
+EARLY = 4
 CHUNKS = 3
 CHUNK = NG // CHUNKS
 
@@ -215,7 +214,7 @@
 
     sources, targets = [], []
     for k in range(2):
-        dy = pick(lax.rem(core * 2 + k + x, 4), (0, 1, 2 - 4 * lax.rem(x, 2), -1))
+        dy = pick(lax.rem(core * 2 + k + x, 4), (0, 1, 2 - 4 * lax.rem(y, 2), -1))
 
         def dz_of(y_hi):
             even = jnp.where(core == 0, 4 * k, 2 - 4 * k)
@@ -341,17 +340,11 @@
         wide = to_lanes(along_lanes(density, right_forward[...]), CHUNK)
         field[at, :] = to_rows(along_rows(wide, left_forward[...]), CHUNK)
 
-    def middle(i, carry):
-        columns = [field[pl.ds(i * ROWS + j, NG, stride=NG), :] for j in range(ROWS)]
-        spectrum = along_rows(jnp.concatenate(columns, axis=1), left_forward[...])
-        at = pl.ds(pl.multiple_of(i * (ROWS * NG), ROWS * NG), ROWS * NG)
-        spectrum = spectrum * to_lanes(kernel[at, :], ROWS)
-        back = along_rows(spectrum, left_backward[...])
-        for j in range(ROWS):
-            field[pl.ds(i * ROWS + j, NG, stride=NG), :] = back[:, j * 128 : (j + 1) * 128]
-        return carry
-
-    lax.fori_loop(0, NG // ROWS, middle, 0)
+    columns = [field[pl.ds(j, NG, stride=NG), :] for j in range(NG)]
+    spectrum = along_rows(jnp.concatenate(columns, axis=1), left_forward[...])
+    back = along_rows(spectrum * to_lanes(kernel[...], NG), left_backward[...])
+    for j in range(NG):
+        field[pl.ds(j, NG, stride=NG), :] = back[:, j * 128 : (j + 1) * 128]
 
     def departure(h, ahead, other):
         return pltpu.make_async_remote_copy(
@@ -365,30 +358,35 @@
 
     low_half = lax.broadcasted_iota(jnp.int32, (NG // 2, 128), 1) < HALF
 
-    for h in range(2):
+    def slabs(h):
         kept_hi = 1 - y_hi if h == 0 else y_hi
-        for pair in ((1, 2), (3, 0)):
-            starts = [
-                pl.multiple_of((lax.rem(x + ahead, 4) * 2 + kept_hi) * (6 * NG), 6 * NG)
-                for ahead in pair
-            ]
-            spectrum = jnp.concatenate([field[pl.ds(at, 6 * NG), :] for at in starts], axis=0)
-            wide = along_rows(to_lanes(spectrum, 12), left_backward[...])
-            potential = along_lanes(to_rows(wide, 12), right_backward[...])
-            for n, (ahead, at) in enumerate(zip(pair, starts)):
-                terms = potential[n * 6 * NG : (n + 1) * 6 * NG] * partner_wide[pl.ds(at, 6 * NG), :]
-                for side in range(2):
-                    planes = []
-                    for i in range(side * 3, side * 3 + 3):
-                        a = terms[i * NG : i * NG + NG // 2]
-                        b = terms[i * NG + NG // 2 : (i + 1) * NG]
-                        swapped = pltpu.roll(jnp.where(low_half, b, a), HALF, 1)
-                        planes.append(jnp.where(low_half, a, b) + swapped)
-                    other = jnp.where(core == side, 0, 1)
-                    partial[h, ahead, other] = packed(jnp.concatenate(planes, axis=0))
-                for other in range(2):
-                    if ahead or other:
-                        departure(h, ahead, other).start()
+        starts = [
+            pl.multiple_of((lax.rem(x + ahead, 4) * 2 + kept_hi) * (6 * NG), 6 * NG)
+            for ahead in range(4)
+        ]
+        spectrum = jnp.concatenate([field[pl.ds(at, 6 * NG), :] for at in starts], axis=0)
+        wide = along_rows(to_lanes(spectrum, 24), left_backward[...])
+        potential = along_lanes(to_rows(wide, 24), right_backward[...])
+        for ahead in (2, 1, 3, 0):
+            terms = (
+                potential[ahead * 6 * NG : (ahead + 1) * 6 * NG]
+                * partner_wide[pl.ds(starts[ahead], 6 * NG), :]
+            )
+            for side in range(2):
+                planes = []
+                for i in range(side * 3, side * 3 + 3):
+                    a = terms[i * NG : i * NG + NG // 2]
+                    b = terms[i * NG + NG // 2 : (i + 1) * NG]
+                    swapped = pltpu.roll(jnp.where(low_half, b, a), HALF, 1)
+                    planes.append(jnp.where(low_half, a, b) + swapped)
+                other = jnp.where(core == side, 0, 1)
+                partial[h, ahead, other] = packed(jnp.concatenate(planes, axis=0))
+            for other in range(2):
+                if ahead or other:
+                    departure(h, ahead, other).start()
+
+    slabs(0)
+    slabs(1)
 
     def gathered(h):
         total = partial[h, 0, 0]

time: 40.9 us -> 39.5 us (0.966)
  the two profiles are of different devices: /device:TPU:1 before, /device:TPU:11 now
where the time goes in v4:
time: 39.5 us; the launch traced here: 39.4 us
  Pallas kernels  38.8 us (98%)
  local copies, waits for them, and re-layouts  0.61 us (2%)
    pallas_call x1, Pallas kernels, on_device(): pl.pallas_call(exchange_kernel, out_shape=jax.ShapeDtypeStruct((3, 1, CEL...  38.8 us

profile of v4, /device:TPU:11, one launch (start us, length us, event | category | flops | bytes accessed | tf_op | source)
XLA Modules:
  0.0 39.4 jit_solution(3759946888288152374)
XLA Ops:
  0.0 38.8 %shard_map.28 = f32[3,1,2304]{2,1,0:T(1,128)S(1)} custom-call(bf16[48,2304]{1,0:T(8,128)(2,1)} %bitcast.3, bf16[608,256]{1,0:T(8,128)(2,1)} %constant.2.clone.table_ref), custom_call_target="tpu_custom_call" | custom-call | tf_op jit(solution)/shard_map/pallas_call | solution.py:430
  38.8 0.6 %copy.4 = f32[1,3,2304]{2,0,1:T(1,128)} copy(f32[1,3,2304]{2,0,1:T(1,128)S(1)} %bitcast.2) | data formatting | bytes 55296

commit v5 on v4

--- a/solution.py
+++ b/solution.py
@@ -193,8 +193,9 @@
 def exchange_kernel(
     own_ref, table_ref, out_ref,
     own, table, spread_ref, partner, own_wide, partner_wide, field, kernel,
-    partial, from_x, row_sum, from_y,
-    planes_ref, copy_sem, in_send, in_recv, x_send, x_recv, y_send, y_recv, opposite_sem, go_sem,
+    partial, from_x, from_far, row_sum, from_y,
+    planes_ref, copy_sem, in_send, in_recv, x_send, x_recv, y_send, y_recv, far_send, far_recv,
+    opposite_sem, far_sem, go_sem,
 ):
     blk = lax.axis_index("blk")
     off = lax.axis_index("off")
@@ -303,6 +304,12 @@
     fill_kernel(kernel)
     load_table.wait()
 
+    pl.semaphore_wait(opposite_sem, 1)
+    for other in range(2):
+        pl.semaphore_signal(
+            far_sem, inc=1, device_id=neighbour(2, other), device_id_type=MESH
+        )
+
     for k in range(2):
 
         @pl.when(defer_to[k])
@@ -353,6 +360,17 @@
             send_sem=x_send.at[h, ahead, other],
             recv_sem=x_recv.at[h, (4 - ahead) % 4, other],
             device_id=neighbour(ahead, other),
+            device_id_type=MESH,
+        )
+
+    def straight(other):
+        cx = lax.rem(x + 2, 4)
+        return pltpu.make_async_remote_copy(
+            src_ref=partial.at[0, 2, other],
+            dst_ref=from_far.at[other],
+            send_sem=far_send.at[other],
+            recv_sem=far_recv.at[other],
+            device_id=(blk, (cx * 2 + 1 - y_hi) * 2 + (1 - core if other else core)),
             device_id_type=MESH,
         )
 
@@ -382,22 +400,25 @@
                 other = jnp.where(core == side, 0, 1)
                 partial[h, ahead, other] = packed(jnp.concatenate(planes, axis=0))
             for other in range(2):
-                if ahead or other:
+                if h == 0 and ahead == 2:
+                    straight(other).start()
+                elif ahead or other:
                     departure(h, ahead, other).start()
 
+    pl.semaphore_wait(far_sem, 2)
     slabs(0)
     slabs(1)
 
     def gathered(h):
         total = partial[h, 0, 0]
-        for ahead, other in around:
+        near = [(ahead, other) for ahead, other in around if h or ahead != 2]
+        for ahead, other in near:
             departure(h, ahead, other).wait()
-        for ahead, other in around:
+        for ahead, other in near:
             total = total + from_x[h, ahead, other]
         return total
 
     row_sum[...] = gathered(0)
-    pl.semaphore_wait(opposite_sem, 1)
     last = pltpu.make_async_remote_copy(
         src_ref=row_sum,
         dst_ref=from_y,
@@ -408,6 +429,9 @@
     )
     last.start()
     kept = gathered(1)
+    for other in range(2):
+        straight(other).wait()
+    kept = kept + (from_far[0] + from_far[1])
 
     for k in range(2):
 
@@ -440,6 +464,7 @@
             wide, wide, wide, wide,
             pltpu.VMEM((2, 4, 2, *slab), F32),
             pltpu.VMEM((2, 4, 2, *slab), F32),
+            pltpu.VMEM((2, *slab), F32),
             pltpu.VMEM(slab, F32),
             pltpu.VMEM(slab, F32),
             pltpu.VMEM((SLAB, 128), F32),
@@ -447,6 +472,8 @@
             dma((2, CHUNKS)), dma((2, CHUNKS)),
             dma((2, 4, 2)), dma((2, 4, 2)),
             dma, dma,
+            dma((2,)), dma((2,)),
+            pltpu.SemaphoreType.REGULAR,
             pltpu.SemaphoreType.REGULAR,
             pltpu.SemaphoreType.REGULAR((2,)),
         ],

time: 39.5 us -> 38.9 us (0.985)
  the two profiles are of different devices: /device:TPU:11 before, /device:TPU:320 now
where the time goes in v5:
time: 38.9 us; the launch traced here: 38.8 us
  Pallas kernels  38.2 us (98%)
  local copies, waits for them, and re-layouts  0.61 us (2%)
    pallas_call x1, Pallas kernels, on_device(): pl.pallas_call(exchange_kernel, out_shape=jax.ShapeDtypeStruct((3, 1, CEL...  38.2 us

profile of v5, /device:TPU:320, one launch (start us, length us, event | category | flops | bytes accessed | tf_op | source)
XLA Modules:
  0.0 38.8 jit_solution(17357389564087687904)
XLA Ops:
  0.0 38.2 %shard_map.28 = f32[3,1,2304]{2,1,0:T(1,128)S(1)} custom-call(bf16[48,2304]{1,0:T(8,128)(2,1)} %bitcast.3, bf16[608,256]{1,0:T(8,128)(2,1)} %constant.2.clone.table_ref), custom_call_target="tpu_custom_call" | custom-call | tf_op jit(solution)/shard_map/pallas_call | solution.py:454
  38.2 0.6 %copy.4 = f32[1,3,2304]{2,0,1:T(1,128)} copy(f32[1,3,2304]{2,0,1:T(1,128)S(1)} %bitcast.2) | data formatting | bytes 55296

commit v6 on v5

--- a/solution.py
+++ b/solution.py
@@ -20,7 +20,7 @@
 HALF = 64
 SLAB = 72
 PACKED = 56
-EARLY = 4
+EARLY = 3
 CHUNKS = 3
 CHUNK = NG // CHUNKS
 
@@ -213,19 +213,24 @@
         z = lax.rem(z + 8, 8)
         return (z * 4 + lax.rem(y, 4), (x * 2 + y // 4) * 2 + core)
 
-    sources, targets = [], []
-    for k in range(2):
-        dy = pick(lax.rem(core * 2 + k + x, 4), (0, 1, 2 - 4 * lax.rem(y, 2), -1))
-
-        def dz_of(y_hi):
-            even = jnp.where(core == 0, 4 * k, 2 - 4 * k)
-            odd = jnp.where(core == 0, 1 - 4 * k, 3 - 4 * k)
-            return jnp.where(y_hi == 0, even, odd)
-
-        sources.append(device(x, y + dy, z + dz_of(y_hi), core))
-        ty = lax.rem(y - dy + 8, 8)
-        targets.append(device(x, ty, z - dz_of(ty // 4), core))
-    itself = (x == 0) & (y_hi == 0) & (core == 0)
+    aside = jnp.where(core == 0, 0, 2 * lax.rem(y, 2) - 1)
+    sign = 1 - 2 * lax.rem(z, 2)
+
+    def dz_of(y_hi):
+        even = jnp.where(core == 0, pick(x, (2, -2, 0, 4)), pick(x, (-2, 2, 4, 0)))
+        odd = jnp.where(core == 0, pick(x, (3, -3, 1, -1)), pick(x, (-1, 1, -3, 3)))
+        return jnp.where(y_hi == 1, even, odd * sign)
+
+    there = lax.rem(y + aside + 8, 8)
+    source = device(x, there, z + dz_of(y_hi), core)
+    dz_there = dz_of(there // 4)
+    target = device(x, there, jnp.where(there // 4 == 1, z - dz_there, z + dz_there), core)
+    mate_y = y + 1 - 2 * lax.rem(y, 2)
+    mate = device(x, mate_y, z, core)
+    mate_source = device(x, mate_y - aside, z + dz_of(y_hi), core)
+    target_z = lax.rem(target[0] // 4, 8)
+    target_mate = device(x, there + 1 - 2 * lax.rem(there, 2), target_z, core)
+    itself = (x == 2) & (y_hi == 1) & (core == 0)
     opposite = (blk, (x * 2 + 1 - y_hi) * 2 + core)
 
     def neighbour(ahead, other):
@@ -245,57 +250,59 @@
     for ahead, other in around:
         greet(neighbour(ahead, other))
 
-    mine_early = z < EARLY
-    moves = (jnp.logical_not(itself), itself | True)
-    to_early = [target[0] // 4 < EARLY for target in targets]
-    from_early = [source[0] // 4 < EARLY for source in sources]
-    defer_to = [moves[k] & mine_early & jnp.logical_not(to_early[k]) for k in range(2)]
-    defer_from = [moves[k] & jnp.logical_not(mine_early) & from_early[k] for k in range(2)]
-    greetings = 9
-    for k in range(2):
-
-        @pl.when(moves[k] & jnp.logical_not(defer_from[k]))
-        def _():
-            greet(sources[k])
-
-        @pl.when(defer_to[k])
-        def _():
-            greet(targets[k])
-
-        greetings = greetings + jnp.where(moves[k] & jnp.logical_not(defer_to[k]), 1, 0)
-        greetings = greetings + jnp.where(defer_from[k], 1, 0)
-
-    pl.semaphore_wait(barrier, greetings)
-
-    for k in range(2):
-
-        @pl.when(defer_from[k])
-        def _():
-            pl.semaphore_signal(
-                go_sem.at[k], inc=1, device_id=sources[k], device_id_type=MESH
-            )
+    moves = jnp.logical_not(itself)
+    early = z < EARLY
+    defer_to = moves & early & (target[0] // 4 >= EARLY)
+    defer_from = moves & jnp.logical_not(early) & (source[0] // 4 < EARLY)
+    double_out = moves & jnp.logical_not(early) & (target_z < EARLY)
+    double_in = moves & early & (source[0] // 4 >= EARLY)
+    greet(mate)
+
+    @pl.when(double_in)
+    def _():
+        greet(mate_source)
+
+    @pl.when(moves & jnp.logical_not(defer_from))
+    def _():
+        greet(source)
+
+    @pl.when(defer_to)
+    def _():
+        greet(target)
+
+    pl.semaphore_wait(
+        barrier,
+        10
+        + jnp.where(moves & jnp.logical_not(defer_to), 1, 0)
+        + jnp.where(defer_from, 1, 0)
+        + jnp.where(double_out, 1, 0),
+    )
+
+    @pl.when(defer_from)
+    def _():
+        pl.semaphore_signal(go_sem, inc=1, device_id=source, device_id_type=MESH)
 
     def arrival(k, c):
         at = pl.ds(c * CHUNK, CHUNK)
+        slot = min(k, 1)
         return pltpu.make_async_remote_copy(
-            src_ref=own_ref.at[at],
-            dst_ref=partner.at[k, at],
+            src_ref=partner.at[0, at] if k == 1 else own_ref.at[at],
+            dst_ref=partner.at[slot, at],
             send_sem=in_send.at[k, c],
-            recv_sem=in_recv.at[k, c],
-            device_id=targets[k],
+            recv_sem=in_recv.at[slot, c],
+            device_id=(target, mate, target_mate)[k],
             device_id_type=MESH,
         )
 
-    later = [
-        moves[k] & jnp.logical_not(mine_early | to_early[k]) & to_early[1 - k]
-        for k in range(2)
-    ]
     for c in range(CHUNKS):
-        for k in range(2):
-
-            @pl.when(moves[k] & jnp.logical_not(defer_to[k] | later[k]))
-            def _():
-                arrival(k, c).start()
+
+        @pl.when(moves & jnp.logical_not(defer_to))
+        def _():
+            arrival(0, c).start()
+
+        @pl.when(double_out)
+        def _():
+            arrival(2, c).start()
 
     pl.semaphore_signal(opposite_sem, inc=1, device_id=below, device_id_type=MESH)
     fill_spread(spread_ref)
@@ -310,20 +317,11 @@
             far_sem, inc=1, device_id=neighbour(2, other), device_id_type=MESH
         )
 
-    for k in range(2):
-
-        @pl.when(defer_to[k])
-        def _():
-            pl.semaphore_wait(go_sem.at[k], 1)
-            for c in range(CHUNKS):
-                arrival(k, c).start()
-
-        @pl.when(later[k])
-        def _():
-            for c in range(CHUNKS):
-                arrival(1 - k, c).wait_send()
-            for c in range(CHUNKS):
-                arrival(k, c).start()
+    @pl.when(defer_to)
+    def _():
+        pl.semaphore_wait(go_sem, 1)
+        for c in range(CHUNKS):
+            arrival(0, c).start()
 
     right_forward = table.at[pl.ds(0, 256)]
     right_backward = table.at[pl.ds(256, 256)]
@@ -334,12 +332,19 @@
     def _():
         partner[0] = own[...]
 
+    def pass_on(c):
+        @pl.when(moves)
+        def _():
+            arrival(0, c).wait_recv()
+
+        @pl.when(jnp.logical_not(double_in))
+        def _():
+            arrival(1, c).start()
+
+    pass_on(0)
     for c in range(CHUNKS):
-
-        @pl.when(moves[0])
-        def _():
-            arrival(0, c).wait_recv()
-
+        if c + 1 < CHUNKS:
+            pass_on(c + 1)
         arrival(1, c).wait_recv()
         spread([(partner.at[0], 0), (partner.at[1], 1)], spread_ref, partner_wide, c * CHUNK, CHUNK)
         at = pl.ds(c * CHUNK * NG, CHUNK * NG)
@@ -433,12 +438,19 @@
         straight(other).wait()
     kept = kept + (from_far[0] + from_far[1])
 
-    for k in range(2):
-
-        @pl.when(moves[k] & jnp.logical_not(later[1 - k]))
-        def _():
-            for c in range(CHUNKS):
-                arrival(k, c).wait_send()
+    for c in range(CHUNKS):
+
+        @pl.when(moves)
+        def _():
+            arrival(0, c).wait_send()
+
+        @pl.when(jnp.logical_not(double_in))
+        def _():
+            arrival(1, c).wait_send()
+
+        @pl.when(double_out)
+        def _():
+            arrival(2, c).wait_send()
 
     last.wait()
     planes_ref[...] = unpacked(F32(-0.25) * (kept + from_y[...]))
@@ -469,13 +481,13 @@
             pltpu.VMEM(slab, F32),
             pltpu.VMEM((SLAB, 128), F32),
             dma((2,)),
-            dma((2, CHUNKS)), dma((2, CHUNKS)),
+            dma((3, CHUNKS)), dma((2, CHUNKS)),
             dma((2, 4, 2)), dma((2, 4, 2)),
             dma, dma,
             dma((2,)), dma((2,)),
             pltpu.SemaphoreType.REGULAR,
             pltpu.SemaphoreType.REGULAR,
-            pltpu.SemaphoreType.REGULAR((2,)),
+            pltpu.SemaphoreType.REGULAR,
         ],
         compiler_params=pltpu.CompilerParams(
             collective_id=0, has_side_effects=True, vmem_limit_bytes=54 * 2**20 - 2**17

time: 38.9 us -> 38.8 us (level)
  the two profiles are of different devices: /device:TPU:320 before, /device:TPU:1 now
where the time goes in v6:
time: 38.8 us; the launch traced here: 38.5 us
  Pallas kernels  37.8 us (97%)
  local copies, waits for them, and re-layouts  0.61 us (2%)
    pallas_call x1, Pallas kernels, on_device(): pl.pallas_call(exchange_kernel, out_shape=jax.ShapeDtypeStruct((3, 1, CEL...  37.8 us

profile of v6, /device:TPU:1, one launch (start us, length us, event | category | flops | bytes accessed | tf_op | source)
XLA Modules:
  0.0 38.5 jit_solution(11488651089205691991)
XLA Ops:
  0.0 37.8 %shard_map.28 = f32[3,1,2304]{2,1,0:T(1,128)S(1)} custom-call(bf16[48,2304]{1,0:T(8,128)(2,1)} %bitcast.3, bf16[608,256]{1,0:T(8,128)(2,1)} %constant.2.clone.table_ref), custom_call_target="tpu_custom_call" | custom-call | tf_op jit(solution)/shard_map/pallas_call | solution.py:466
  37.8 0.6 %copy.4 = f32[1,3,2304]{2,0,1:T(1,128)} copy(f32[1,3,2304]{2,0,1:T(1,128)S(1)} %bitcast.2) | data formatting | bytes 55296

commit v7 on v6

--- a/solution.py
+++ b/solution.py
@@ -390,7 +390,7 @@
         spectrum = jnp.concatenate([field[pl.ds(at, 6 * NG), :] for at in starts], axis=0)
         wide = along_rows(to_lanes(spectrum, 24), left_backward[...])
         potential = along_lanes(to_rows(wide, 24), right_backward[...])
-        for ahead in (2, 1, 3, 0):
+        for ahead in (1, 3, 0, 2):
             terms = (
                 potential[ahead * 6 * NG : (ahead + 1) * 6 * NG]
                 * partner_wide[pl.ds(starts[ahead], 6 * NG), :]

time: 38.8 us -> 38.3 us (0.987)
  Pallas kernels: 37.8 us -> 37.3 us
    pallas_call x1, Pallas kernels: 37.8 us -> 37.3 us  [on_device(): pl.pallas_call(exchange_kernel, out_shape=jax.ShapeDtypeStruct((3, 1, CEL...]
where the time goes in v7:
time: 38.3 us; the launch traced here: 37.9 us
  Pallas kernels  37.3 us (97%)
  local copies, waits for them, and re-layouts  0.61 us (2%)
    pallas_call x1, Pallas kernels, on_device(): pl.pallas_call(exchange_kernel, out_shape=jax.ShapeDtypeStruct((3, 1, CEL...  37.3 us

profile of v7, /device:TPU:1, one launch (start us, length us, event | category | flops | bytes accessed | tf_op | source)
XLA Modules:
  0.0 37.9 jit_solution(334324752631841841)
XLA Ops:
  0.0 37.3 %shard_map.28 = f32[3,1,2304]{2,1,0:T(1,128)S(1)} custom-call(bf16[48,2304]{1,0:T(8,128)(2,1)} %bitcast.3, bf16[608,256]{1,0:T(8,128)(2,1)} %constant.2.clone.table_ref), custom_call_target="tpu_custom_call" | custom-call | tf_op jit(solution)/shard_map/pallas_call | solution.py:466
  37.3 0.6 %copy.4 = f32[1,3,2304]{2,0,1:T(1,128)} copy(f32[1,3,2304]{2,0,1:T(1,128)S(1)} %bitcast.2) | data formatting | bytes 55296

commit v8 on v7

--- a/solution.py
+++ b/solution.py
@@ -20,7 +20,7 @@
 HALF = 64
 SLAB = 72
 PACKED = 56
-EARLY = 3
+EARLY = 4
 CHUNKS = 3
 CHUNK = NG // CHUNKS
 

time: 38.3 us -> 38.3 us (level)
  no operation moved by 1% of the time
where the time goes in v8:
time: 38.3 us; the launch traced here: 38 us
  Pallas kernels  37.4 us (98%)
  local copies, waits for them, and re-layouts  0.61 us (2%)
    pallas_call x1, Pallas kernels, on_device(): pl.pallas_call(exchange_kernel, out_shape=jax.ShapeDtypeStruct((3, 1, CEL...  37.4 us

profile of v8, /device:TPU:1, one launch (start us, length us, event | category | flops | bytes accessed | tf_op | source)
XLA Modules:
  0.0 38.0 jit_solution(8165816543652677354)
XLA Ops:
  0.0 37.4 %shard_map.28 = f32[3,1,2304]{2,1,0:T(1,128)S(1)} custom-call(bf16[48,2304]{1,0:T(8,128)(2,1)} %bitcast.3, bf16[608,256]{1,0:T(8,128)(2,1)} %constant.2.clone.table_ref), custom_call_target="tpu_custom_call" | custom-call | tf_op jit(solution)/shard_map/pallas_call | solution.py:466
  37.4 0.6 %copy.4 = f32[1,3,2304]{2,0,1:T(1,128)} copy(f32[1,3,2304]{2,0,1:T(1,128)S(1)} %bitcast.2) | data formatting | bytes 55296
